TPU v7x, 32 devices: a whole 2x2x4 slice. The times are simulated.
32 devices in a mesh: ctx: 8 (over z, core), vocab: 4 (over y, x).
Axes of the slice: x: 2, y: 2, z: 4, core: 2. Of those that a mesh axis runs over, the one named last changes fastest.
Arguments:
- hidden_in: bfloat16 [1024, 4096], P('ctx'), may hold values from -128 to 128
- attn_gain: float32 [4096], replicated, may hold values from 0.1 to 1.9
- w_query: bfloat16 [4096, 4096], P(None, 'vocab'), may hold values from -2 to 2
- w_key: bfloat16 [4096, 1024], P(None, 'vocab'), may hold values from -2 to 2
- w_value: bfloat16 [4096, 1024], P(None, 'vocab'), may hold values from -0.09375 to 0.09375
- w_out: bfloat16 [4096, 4096], P('vocab'), may hold values from -0.5 to 0.5
- final_gain: float32 [4096], replicated, may hold values from 0.5 to 1.5
- teacher_head: bfloat16 [65536, 4096], P(('vocab', 'ctx')), may hold values from -18 to 18
- draft_rows: bfloat16 [1024, 2048], P('ctx'), may hold values from -1.5 to 1.5
- draft_head: bfloat16 [65536, 2048], P(('vocab', 'ctx')), may hold values from -64 to 64
- target_ids: int32 [1024], replicated, may hold values from 0 to 65535
- rollout_lengths: int32 [4], replicated, may hold values from 1 to 512, 1024 in all
- stretch_order: int32 [16], replicated, may hold values from 0 to 15, as said below
Outputs:
- draft_grad: float32 [1024, 2048], P('ctx', 'vocab')
Inputs may be any that keep to these rules, and one draw needn't show every extreme that they name: `rollout_lengths`: the lengths add up to 1024. `stretch_order`: each block number appears once; entries 2c and 2c + 1 add up to 15.
All inputs are finite; a program needn't handle non-finite values.
Results may differ from a plain program's by a relative error of at most 0.0045.
Values may be sent and summed in bfloat16 or wider, within the bound.
A program may use at most 128 MiB of HBM per device.

v0:
```python
import jax
import jax.numpy as jnp
from jax import lax
from jax.sharding import PartitionSpec as P

HEAD_DIM = 128


EPSILON = 1e-05
ROPE_BASE = 500000.0
MIXING = 0.5
NEGATIVE = -1e30


def joined(part, axis, combine):
    gathered = jax.tree.map(lambda a: lax.all_gather(a, axis), part)

    def take(source):
        return jax.tree.map(lambda a: lax.dynamic_index_in_dim(a, source, 0, False), gathered)

    return lax.fori_loop(
        1, lax.axis_size(axis), lambda source, state: combine(state, take(source)), take(0)
    )


def rms_scale(values, gain):
    mean_square = jnp.mean(values * values, axis=-1, keepdims=True)
    return values * lax.rsqrt(mean_square + EPSILON) * gain


def rotate(vectors, positions):
    half_dim = vectors.shape[-1] // 2
    exponents = jnp.arange(half_dim, dtype=jnp.float32) * (2.0 / vectors.shape[-1])
    frequencies = jnp.power(ROPE_BASE, -exponents)
    angles = positions.astype(jnp.float32)[:, None] * frequencies[None, :]
    cosine_values = jnp.cos(angles)[:, None, :]
    sine_values = jnp.sin(angles)[:, None, :]
    leading = vectors[..., :half_dim]
    trailing = vectors[..., half_dim:]
    return jnp.concatenate(
        [
            leading * cosine_values - trailing * sine_values,
            trailing * cosine_values + leading * sine_values,
        ],
        axis=-1,
    )


def combine_pairs(former, latter):
    merged = []
    for member in range(0, len(former), 2):
        highest = jnp.maximum(former[member], latter[member])
        summed = former[member + 1] * jnp.exp(former[member] - highest) + latter[
            member + 1
        ] * jnp.exp(latter[member] - highest)
        merged = merged + [highest, summed]
    return tuple(merged)


def local_totals(logits):
    highest = jnp.max(logits, axis=1)
    return (highest, jnp.sum(jnp.exp(logits - highest[:, None]), axis=1))


def on_device(
    hidden_in,
    attn_gain,
    w_query,
    w_key,
    w_value,
    w_out,
    final_gain,
    teacher_head,
    draft_rows,
    draft_head,
    target_ids,
    rollout_lengths,
    stretch_order,
):
    row_count = hidden_in.shape[0]
    head_dim = HEAD_DIM
    local_heads = w_query.shape[1] // head_dim
    local_groups = w_key.shape[1] // head_dim
    group_size = local_heads // local_groups
    ctx_count = lax.axis_size("ctx")
    half_rows = row_count // 2
    stretch_ids = jnp.arange(stretch_order.shape[0], dtype=jnp.int32)
    rollout_ends = jnp.cumsum(rollout_lengths)

    def locate(begin_row, span_rows):
        row_ids = begin_row + jnp.arange(span_rows, dtype=jnp.int32)
        stretch_hit = (row_ids // half_rows)[:, None] == stretch_ids[None, :]
        stretch_start = jnp.sum(jnp.where(stretch_hit, stretch_order[None, :], 0), axis=1)
        positions = stretch_start * half_rows + row_ids % half_rows
        rollouts = jnp.sum((positions[:, None] >= rollout_ends[None, :]).astype(jnp.int32), axis=1)
        return (positions, rollouts)

    query_pos, query_roll = locate(lax.axis_index("ctx") * row_count, row_count)
    normed = rms_scale(hidden_in.astype(jnp.float32), attn_gain).astype(jnp.bfloat16)
    queries = jnp.dot(normed, w_query, preferred_element_type=jnp.float32).reshape(
        row_count, local_heads, head_dim
    )
    queries = (
        rotate(queries, query_pos)
        .astype(jnp.bfloat16)
        .reshape(row_count, local_groups, group_size, head_dim)
    )
    keys = jnp.dot(normed, w_key, preferred_element_type=jnp.float32).reshape(
        row_count, local_groups, head_dim
    )
    keys = rotate(keys, query_pos).astype(jnp.bfloat16).reshape(row_count, local_groups * head_dim)
    values = jnp.dot(normed, w_value, preferred_element_type=jnp.float32).astype(jnp.bfloat16)
    score_scale = head_dim ** (-0.5)
    pieces = (
        lax.all_gather(keys, "ctx", axis=0, tiled=True),
        lax.all_gather(values, "ctx", axis=0, tiled=True),
    )
    key_piece = pieces[0].reshape(-1, local_groups, head_dim)
    value_piece = pieces[1].reshape(-1, local_groups, head_dim)
    key_count = key_piece.shape[0]
    key_pos, key_roll = locate(jnp.int32(0), key_count)
    allowed = (key_pos[None, :] <= query_pos[:, None]) & (key_roll[None, :] == query_roll[:, None])
    running_max = jnp.full((row_count, local_groups, group_size), NEGATIVE, jnp.float32)
    visible = allowed[:, None, None, :]
    scores = (
        jnp.einsum("tkgd,nkd->tkgn", queries, key_piece, preferred_element_type=jnp.float32)
        * score_scale
    )
    scores = jnp.where(visible, scores, NEGATIVE)
    new_max = jnp.maximum(running_max, jnp.max(scores, axis=-1))
    weights = jnp.where(visible, jnp.exp(scores - new_max[..., None]), 0.0)
    new_sum = jnp.sum(weights, axis=-1)
    new_weighted = jnp.einsum(
        "tkgn,nkd->tkgd",
        weights.astype(jnp.bfloat16),
        value_piece,
        preferred_element_type=jnp.float32,
    )
    attended = (
        (new_weighted / new_sum[..., None])
        .astype(jnp.bfloat16)
        .reshape(row_count, local_heads * head_dim)
    )
    partial_value = jnp.dot(attended, w_out, preferred_element_type=jnp.float32)
    mixed = hidden_in.astype(jnp.float32) + lax.psum(partial_value, "vocab")
    final = rms_scale(mixed, final_gain).astype(jnp.bfloat16)
    word_count = teacher_head.shape[0]
    pieces = (
        lax.all_gather(final, "ctx", axis=0, tiled=True),
        lax.all_gather(draft_rows, "ctx", axis=0, tiled=True),
    )
    teacher_part = jnp.einsum(
        "nd,wd->nw", pieces[0], teacher_head, preferred_element_type=jnp.float32
    )
    draft_part = jnp.einsum("nd,wd->nw", pieces[1], draft_head, preferred_element_type=jnp.float32)
    teacher_max, teacher_sum = local_totals(teacher_part)
    draft_max, draft_sum = local_totals(draft_part)
    totals = joined(
        (teacher_max, teacher_sum, draft_max, draft_sum), ("ctx", "vocab"), combine_pairs
    )
    teacher_probs = jnp.exp(teacher_part - totals[0][:, None]) / totals[1][:, None]
    draft_probs = jnp.exp(draft_part - totals[2][:, None]) / totals[3][:, None]
    word_start = (lax.axis_index("vocab") * ctx_count + lax.axis_index("ctx")) * word_count
    word_ids = word_start + jnp.arange(word_count, dtype=jnp.int32)
    soft = (1.0 - MIXING) * teacher_probs + jnp.where(
        target_ids[:, None] == word_ids[None, :], MIXING, 0.0
    )
    delta = (draft_probs - soft).astype(jnp.bfloat16)
    reduced = lax.psum_scatter(
        jnp.dot(delta, draft_head, preferred_element_type=jnp.float32),
        "ctx",
        scatter_dimension=0,
        tiled=True,
    )
    return lax.psum_scatter(reduced, "vocab", scatter_dimension=1, tiled=True)


def solution(mesh):
    placed = (
        P("ctx", None),
        P(),
        P(None, "vocab"),
        P(None, "vocab"),
        P(None, "vocab"),
        P("vocab", None),
        P(),
        P(("vocab", "ctx"), None),
        P("ctx", None),
        P(("vocab", "ctx"), None),
        P(),
        P(),
        P(),
    )
    return jax.shard_map(
        on_device, mesh=mesh, in_specs=placed, out_specs=P("ctx", "vocab"), check_vma=False
    )
```

profile of v0, /device:TPU:0, one launch (start us, length us, event | category | flops | bytes accessed | tf_op | source)
XLA Modules:
  0.0 591.6 jit_solution(5776366497063500067)
XLA Ops:
  7.4 0.0 copy-start
  7.4 0.0 all-reduce.2.cloned.1.call-start
  7.4 1.7 fusion.4
  9.1 0.7 select_reduce_fusion.1
  9.9 0.7 select_reduce_fusion
  10.6 0.8 reduce-window.8
  11.5 0.1 convert_reduce_fusion.1
  11.5 0.1 convert_reduce_fusion
  11.6 0.0 copy-done
  11.6 1.7 convolution_convert_fusion
  13.4 0.0 copy-done.2
  13.4 0.0 copy-done.7
  13.4 2.1 fusion.39
  15.5 0.1 reshape.264
  15.5 0.3 multiply_cosine_fusion
  15.9 0.3 subtract_convert_fusion.3
  16.1 0.2 pad_maximum_fusion
  16.3 0.1 copy.30
  16.5 15.4 %all_gather.38 = bf16[1024,256]{0,1:T(8,128)(2,1)S(1)} all-gather(bf16[128,256]{0,1:T(8,128)(2,1)S(1)} %bitcast.78), channel_id=1, replica_groups=mesh['ctx'=8,'vocab'=4] {'ctx'}, dimensions={0}, use_global_device_ids=true | all-gather | bytes 589824 | tf_op jit(solution)/shard_map/all_gather | solution.py:115
  31.9 14.7 %all_gather.37 = bf16[1024,256]{1,0:T(8,128)(2,1)S(1)} all-gather(bf16[128,256]{1,0:T(8,128)(2,1)S(1)} %convolution_convert_fusion), channel_id=1, replica_groups=mesh['ctx'=8,'vocab'=4] {'ctx'}, dimensions={0}, use_global_device_ids=true | all-gather | bytes 589824 | tf_op jit(solution)/shard_map/all_gather | solution.py:116
  46.6 1.0 copy.39
  47.6 4.7 convolution_bitcast_fusion
  52.3 0.1 copy.42
  52.4 0.3 subtract_convert_fusion.2
  52.8 0.3 compare_and_fusion
  53.1 0.0 slice-start
  53.1 1.0 fusion.1
  54.1 1.0 fusion.2
  55.1 0.0 slice-start.1
  55.2 1.2 fusion.16
  56.3 1.1 slice-done.1
  57.4 2.6 fusion.46
  60.0 0.0 all-reduce.2.cloned.1.call-update
  60.0 0.0 all-gather.7.cloned.1.call-start
  60.1 0.5 all-gather.7.cloned.1.call-update
  60.6 0.0 all-gather.9.cloned.1.call-start
  60.7 69.2 %all-reduce.2.cloned.1.call-done = f32[128,4096]{1,0:T(8,128)} async-done(((f32[128,4096]{1,0:T(8,128)}), f32[128,4096]{1,0:T(8,128)}) %all-reduce.2.cloned.1.call-update) | async-done | bytes 2097168 | tf_op jit(solution)/shard_map/psum | solution.py:145
  129.8 2.1 multiply_reduce_fusion
  131.9 0.0 copy-done.8
  131.9 0.1 copy-done.3
  132.1 1.4 multiply_convert_fusion
  133.5 0.0 all-gather.9.cloned.1.call-update
  133.5 0.2 reduce-scatter.3.cloned.1.call-start
  133.7 0.0 all-gather.7.cloned.1.call-done
  133.8 14.6 %fusion.45 = (f32[1024]{0:T(1024)S(1)}, f32[1024,2048]{1,0:T(8,128)}) fusion(bf16[1024,2048]{1,0:T(8,128)(2,1)} %all-gather.7.cloned.1.call-done, bf16[2048,2048]{1,0:T(8,128)(2,1)} %param.24), kind=kOutput, calls=%fused_computation.81 | convolution fusion | flops 8592030720 | bytes 20975616 | tf_op jit(solution)/shard_map/nd,wd->nw/dot_general | solution.py:155
  148.4 69.9 %all-gather.2 = f32[32768]{0:T(1024)S(1)} all-gather(f32[1024]{0:T(1024)S(1)} %get-tuple-element.268), channel_id=4, replica_groups=mesh['ctx'=8,'vocab'=4] {'ctx','vocab'}, dimensions={0}, use_global_device_ids=true | all-gather | bytes 135168 | tf_op jit(solution)/shard_map/all_gather | solution.py:16
  218.3 4.7 exponential_reduce_fusion
  223.0 64.3 %all-gather.3 = f32[32768]{0:T(1024)S(1)} all-gather(f32[1024]{0:T(1024)S(1)} %exponential_reduce_fusion), channel_id=5, replica_groups=mesh['ctx'=8,'vocab'=4] {'ctx','vocab'}, dimensions={0}, use_global_device_ids=true | all-gather | bytes 135168 | tf_op jit(solution)/shard_map/all_gather | solution.py:16
  287.3 0.0 all-gather.9.cloned.1.call-done
  287.3 24.3 %fusion.44 = (f32[1024]{0:T(1024)S(1)}, f32[1024,2048]{1,0:T(8,128)}) fusion(bf16[1024,4096]{1,0:T(8,128)(2,1)} %all-gather.9.cloned.1.call-done, bf16[2048,4096]{1,0:T(8,128)(2,1)} %param.22), kind=kOutput, calls=%fused_computation.80 | convolution fusion | flops 17181966336 | bytes 33558528 | tf_op jit(solution)/shard_map/nd,wd->nw/dot_general | solution.py:152
  311.7 66.5 %all-gather = f32[32768]{0:T(1024)S(1)} all-gather(f32[1024]{0:T(1024)S(1)} %get-tuple-element.266), channel_id=2, replica_groups=mesh['ctx'=8,'vocab'=4] {'ctx','vocab'}, dimensions={0}, use_global_device_ids=true | all-gather | bytes 135168 | tf_op jit(solution)/shard_map/all_gather | solution.py:16
  378.2 0.0 slice-start.2
  378.2 0.0 slice-start.3
  378.2 0.0 copy-start.9
  378.2 4.6 exponential_reduce_fusion.1
  382.8 64.3 %all-gather.1 = f32[32768]{0:T(1024)S(1)} all-gather(f32[1024]{0:T(1024)S(1)} %exponential_reduce_fusion.1), channel_id=3, replica_groups=mesh['ctx'=8,'vocab'=4] {'ctx','vocab'}, dimensions={0}, use_global_device_ids=true | all-gather | bytes 135168 | tf_op jit(solution)/shard_map/all_gather | solution.py:16
  447.2 3.9 while.21
  451.1 0.0 copy-done.9
  451.2 18.9 %fusion = f32[1024,2048]{1,0:T(8,128)} fusion(bf16[2048,2048]{1,0:T(8,128)(2,1)} %param.24, f32[1024,2048]{1,0:T(8,128)} %get-tuple-element.267, f32[1024,2048]{1,0:T(8,128)} %get-tuple-element.269, s32[2048]{0:T(1024)S(1)} %iota_add_fusion, f32[1024]{0:T(1024)S(1)} %get-tuple-element.231, f32[1024]{0:T(1024)S(1)} %get-tuple-element.230, ...), kind=kOutput, calls=%fused_computation.11 | convolution fusion | flops 8610906112 | bytes 33583104 | tf_op jit(solution)/shard_map/dot_general | solution.py:170
  470.0 0.0 reduce-scatter.3.cloned.1.call-update
  470.0 0.0 reduce-scatter.5.cloned.1.call-start
  470.1 87.5 %reduce-scatter.3.cloned.1.call-done = f32[128,2048]{1,0:T(8,128)} async-done(((f32[1024,2048]{1,0:T(8,128)}), f32[128,2048]{1,0:T(8,128)}) %reduce-scatter.3.cloned.1.call-update) | async-done | bytes 1048592 | tf_op jit(solution)/shard_map/reduce_scatter | solution.py:169
  557.6 0.0 reduce-scatter.5.cloned.1.call-update
  557.6 26.3 %reduce-scatter.5.cloned.1.call-done = f32[128,512]{1,0:T(8,128)} async-done(((f32[128,2048]{1,0:T(8,128)}), f32[128,512]{1,0:T(8,128)}) %reduce-scatter.5.cloned.1.call-update) | async-done | bytes 262160 | tf_op jit(solution)/shard_map/reduce_scatter | solution.py:175
  (188 shorter events, 2.4 us)
Async XLA Ops:
  7.4 4.3 copy-start
  7.4 6.0 %copy-start.2 = (bf16[128,4096]{1,0:T(8,128)(2,1)S(1)}, bf16[128,4096]{1,0:T(8,128)(2,1)}, u32[]{:S(2)}) copy-start(bf16[128,4096]{1,0:T(8,128)(2,1)} %param.15) | copy-start | bytes 3145732
  7.4 6.0 %copy-start.7 = (f32[4096]{0:T(1024)S(1)}, f32[4096]{0:T(1024)}, u32[]{:S(2)}) copy-start(f32[4096]{0:T(1024)} %param.16) | copy-start | bytes 49156
  7.4 122.5 %all-reduce.2.cloned.1.call-start = ((), (), s32[]{:S(2)}) async-start(), calls=%async_computation.3 | async-start | bytes 4194304 | tf_op jit(solution)/shard_map/psum | solution.py:145
  53.1 2.0 copy-start.6
  53.1 3.2 slice-start
  55.1 2.3 slice-start.1
  60.0 71.9 %copy-start.8 = (f32[4096]{0:T(1024)S(1)}, f32[4096]{0:T(1024)}, u32[]{:S(2)}) copy-start(f32[4096]{0:T(1024)} %param.21) | copy-start | bytes 49156
  60.0 73.7 %all-gather.7.cloned.1.call-start = ((), (), s32[]{:S(2)}) async-start(), calls=%async_computation.2 | async-start | bytes 4718592 | tf_op jit(solution)/shard_map/all_gather | solution.py:150
  60.6 226.7 %all-gather.9.cloned.1.call-start = ((), (), s32[]{:S(2)}) async-start(), calls=%async_computation.4 | async-start | bytes 9437184 | tf_op jit(solution)/shard_map/all_gather | solution.py:149
  129.8 2.2 copy-start.3
  133.5 424.1 %reduce-scatter.3.cloned.1.call-start = ((), (), s32[]{:S(2)}) async-start(), calls=%async_computation.5 | async-start | bytes 9437184 | tf_op jit(solution)/shard_map/reduce_scatter | solution.py:169
  218.3 4.7 copy-start.5
  287.3 24.4 %copy-start.4 = (f32[32768]{0:T(1024)}, f32[32768]{0:T(1024)S(1)}, u32[]{:S(2)}) copy-start(f32[32768]{0:T(1024)S(1)} %all-gather.3) | copy-start | bytes 393220
  378.2 69.1 %slice-start.2 = ((f32[32768]{0:T(1024)}), f32[1024]{0:T(1024)S(1)}, s32[]{:S(2)}) async-start(f32[32768]{0:T(1024)} %copy-done.4), calls=%async_computation.9 | async-start | bytes 8192 | tf_op jit(solution)/shard_map/jit(dynamic_index_in_dim)/dynamic_slice | solution.py:19
  378.2 69.0 %slice-start.3 = ((f32[32768]{0:T(1024)}), f32[1024]{0:T(1024)S(1)}, s32[]{:S(2)}) async-start(f32[32768]{0:T(1024)} %copy-done.5), calls=%async_computation.10 | async-start | bytes 8192 | tf_op jit(solution)/shard_map/jit(dynamic_index_in_dim)/dynamic_slice | solution.py:19
  378.2 73.0 %copy-start.9 = (s32[1024]{0:T(1024)S(1)}, s32[1024]{0:T(1024)}, u32[]{:S(2)}) copy-start(s32[1024]{0:T(1024)} %param.25) | copy-start | bytes 12292
  470.0 114.0 %copy-start.1 = (bf16[4096,256]{1,0:T(8,128)(2,1)S(1)}, bf16[4096,256]{1,0:T(8,128)(2,1)}, u32[]{:S(2)}) copy-start(bf16[4096,256]{1,0:T(8,128)(2,1)} %param.19) | copy-start | bytes 6291460
  470.0 113.9 %reduce-scatter.5.cloned.1.call-start = ((), (), s32[]{:S(2)}) async-start(), calls=%async_computation.6 | async-start | bytes 1310720 | tf_op jit(solution)/shard_map/reduce_scatter | solution.py:175
Sparse Core Ops, SparseCore 0:
  60.1 69.6 all-reduce.1
  557.7 26.1 reduce-scatter.4
Sparse Core Ops, SparseCore 1:
  62.2 46.7 all-gather.6
  133.6 82.3 all-gather.8
  470.1 87.4 reduce-scatter.2
where the time goes:
time: 592 us
  blocking collectives  295 us (50%)
  waiting for transfers between devices  184 us (31%)
  matrix products  71 us (12%)
  other arithmetic  19.9 us (3%)
  between operations  15.4 us (3%)
    all_gather x4, blocking collectives, joined(): gathered = jax.tree.map(lambda a: lax.all_gather(a, axis), part)  265 us
    reduce_scatter x1, waiting for transfers between devices, on_device(): lax.psum_scatter(jnp.dot(delta, draft_head, preferred_element_type=jnp.fl...  87.5 us
    psum x1, waiting for transfers between devices, on_device(): mixed = hidden_in.astype(jnp.float32) + lax.psum(partial_value, 'vocab')  69.2 us
    reduce_scatter x1, waiting for transfers between devices, on_device(): return lax.psum_scatter(reduced, 'vocab', scatter_dimension=1, tiled=True)  26.3 us
    dot_general x1, matrix products, on_device(): jnp.einsum('nd,wd->nw', pieces[0], teacher_head, preferred_element_type=j...  24.3 us
    dot_general x1, matrix products, on_device(): jnp.dot(delta, draft_head, preferred_element_type=jnp.float32)  18.9 us
    all_gather x1, blocking collectives, on_device(): lax.all_gather(keys, 'ctx', axis=0, tiled=True)  15.4 us
    all_gather x1, blocking collectives, on_device(): lax.all_gather(values, 'ctx', axis=0, tiled=True)  14.7 us
  transfers between devices with their start and end apart: 5, of which 3 were waited for; matrix products, arithmetic and copies ran while one was open for 4% of the time, Pallas kernels for 0%

commit v1 on v0

--- a/solution.py
+++ b/solution.py
@@ -1,6 +1,10 @@
+import functools
+
 import jax
 import jax.numpy as jnp
 from jax import lax
+from jax.experimental import pallas as pl
+from jax.experimental.pallas import tpu as pltpu
 from jax.sharding import PartitionSpec as P
 
 HEAD_DIM = 128
@@ -10,17 +14,6 @@
 ROPE_BASE = 500000.0
 MIXING = 0.5
 NEGATIVE = -1e30
-
-
-def joined(part, axis, combine):
-    gathered = jax.tree.map(lambda a: lax.all_gather(a, axis), part)
-
-    def take(source):
-        return jax.tree.map(lambda a: lax.dynamic_index_in_dim(a, source, 0, False), gathered)
-
-    return lax.fori_loop(
-        1, lax.axis_size(axis), lambda source, state: combine(state, take(source)), take(0)
-    )
 
 
 def rms_scale(values, gain):
@@ -46,15 +39,305 @@
     )
 
 
+MESH = pl.DeviceIdType.MESH
+VMEM_LIMIT = 56 * 1024 * 1024
+
+
+def place():
+    ctx = lax.axis_index("ctx")
+    core = ctx % 2
+    return ctx, lax.axis_index("vocab"), core, ctx // 2, ctx + 1 - 2 * core
+
+
+def flip(index, mask):
+    bit = 1
+    while bit <= mask:
+        if mask & bit:
+            index = index + bit * (1 - 2 * ((index // bit) % 2))
+        bit *= 2
+    return index
+
+
+def greet(devices):
+    barrier = pltpu.get_barrier_semaphore()
+    for device in devices:
+        pl.semaphore_signal(barrier, inc=1, device_id=device, device_id_type=MESH)
+    pl.semaphore_wait(barrier, len(devices))
+
+
+def push(source, target, send, recv, device):
+    return pltpu.make_async_remote_copy(
+        src_ref=source,
+        dst_ref=target,
+        send_sem=send,
+        recv_sem=recv,
+        device_id=device,
+        device_id_type=MESH,
+    )
+
+
+def spread(chips, peers, block, sems):
+    ctx, vocab, core, chip, sibling = place()
+    z_send, z_recv, v_send, v_recv, s_send, s_recv = sems
+    bits = [1 << i for i in range(peers.bit_length() - 1)]
+    orders = (bits, bits[::-1])
+    sent = []
+
+    def hand_on(far, mask, half):
+        source = ((chip - far + chips) % chips) * 2 + core
+        piece = block(source, flip(vocab, mask), half)
+        reached = [i for i, bit in enumerate(orders[half]) if mask & bit]
+        begin = reached[-1] + 1 if reached else 0
+        for i in range(begin, len(bits)):
+            bit = orders[half][i]
+            sent.append(
+                push(
+                    piece,
+                    piece,
+                    v_send.at[far, half, mask, i],
+                    v_recv.at[far, half, mask | bit],
+                    (ctx, flip(vocab, bit)),
+                )
+            )
+            sent[-1].start()
+        sent.append(
+            push(
+                piece,
+                piece,
+                s_send.at[far, half, mask],
+                s_recv.at[far, half, mask],
+                (sibling, vocab),
+            )
+        )
+        sent[-1].start()
+
+    own = [block(ctx, vocab, half) for half in (0, 1)]
+    for half in (0, 1):
+        for far in range(1, chips):
+            sent.append(
+                push(
+                    own[half],
+                    own[half],
+                    z_send.at[far, half],
+                    z_recv.at[far, half],
+                    (((chip + far) % chips) * 2 + core, vocab),
+                )
+            )
+            sent[-1].start()
+        hand_on(0, 0, half)
+    for step in range(1, chips + len(bits)):
+        for level in range(0, len(bits) + 1):
+            far = step - level
+            if not 0 <= far < chips or (far == 0 and level == 0):
+                continue
+            for half in (0, 1):
+                for mask in [m for m in range(peers) if bin(m).count("1") == level]:
+                    source = ((chip - far + chips) % chips) * 2 + core
+                    piece = block(source, flip(vocab, mask), half)
+                    sem = v_recv.at[far, half, mask] if mask else z_recv.at[far, half]
+                    push(piece, piece, sem, sem, (sibling, vocab)).wait_recv()
+                    hand_on(far, mask, half)
+    for far in range(chips):
+        for half in (0, 1):
+            for mask in range(peers):
+                source = ((chip - far + chips) % chips) * 2 + 1 - core
+                piece = block(source, flip(vocab, mask), half)
+                sem = s_recv.at[far, half, mask]
+                push(piece, piece, sem, sem, (sibling, vocab)).wait_recv()
+    for copy in sent:
+        copy.wait_send()
+
+
+def spread_sems(chips, peers):
+    dma = pltpu.SemaphoreType.DMA
+    depth = max(1, peers.bit_length() - 1)
+    return [
+        dma((chips, 2)),
+        dma((chips, 2)),
+        dma((chips, 2, peers, depth)),
+        dma((chips, 2, peers)),
+        dma((chips, 2, peers)),
+        dma((chips, 2, peers)),
+    ]
+
+
+def communicate(body, out_shape, operands, scratch, collective):
+    return pl.pallas_call(
+        body,
+        out_shape=out_shape,
+        in_specs=[pl.BlockSpec(memory_space=pltpu.VMEM)] * len(operands),
+        out_specs=pl.BlockSpec(memory_space=pltpu.VMEM),
+        scratch_shapes=scratch,
+        compiler_params=pltpu.CompilerParams(
+            collective_id=collective, has_side_effects=True, vmem_limit_bytes=VMEM_LIMIT
+        ),
+    )(*operands)
+
+
+def gather_context_body(chips, own_ref, out_ref, *sems):
+    ctx, vocab, core, chip, sibling = place()
+    width = own_ref.shape[1] // 2
+    greet(
+        [(sibling, vocab)]
+        + [(((chip + far) % chips) * 2 + core, vocab) for far in range(1, chips)]
+    )
+    out_ref[ctx] = own_ref[...]
+    spread(
+        chips, 1, lambda c, v, half: out_ref.at[c, :, half * width : (half + 1) * width], sems
+    )
+
+
+def mix_and_gather_body(
+    chips, peers, part_ref, hidden_ref, gain_ref, out_ref, send_buf, recv_buf, r_send, r_recv, *sems
+):
+    ctx, vocab, core, chip, sibling = place()
+    width = part_ref.shape[2] // 2
+    greet(
+        [(sibling, vocab)]
+        + [(((chip + far) % chips) * 2 + core, vocab) for far in range(1, chips)]
+        + [(ctx, (vocab + far) % peers) for far in range(1, peers)]
+    )
+    copies = []
+    for far in range(1, peers):
+        owner = (vocab + far) % peers
+        send_buf[far - 1] = part_ref[owner].astype(jnp.bfloat16)
+        copies.append(
+            push(
+                send_buf.at[far - 1],
+                recv_buf.at[far - 1],
+                r_send.at[far - 1],
+                r_recv.at[far - 1],
+                (ctx, owner),
+            )
+        )
+        copies[-1].start()
+    for copy in copies:
+        copy.wait_recv()
+    mixed = hidden_ref[vocab].astype(jnp.float32) + part_ref[vocab]
+    for far in range(1, peers):
+        mixed = mixed + recv_buf[far - 1].astype(jnp.float32)
+    out_ref[ctx, vocab] = rms_scale(mixed, gain_ref[...]).astype(jnp.bfloat16)
+    spread(
+        chips,
+        peers,
+        lambda c, v, half: out_ref.at[c, v, :, half * width : (half + 1) * width],
+        sems,
+    )
+    for copy in copies:
+        copy.wait_send()
+
+
 def combine_pairs(former, latter):
     merged = []
-    for member in range(0, len(former), 2):
+    for member in (0, 2):
         highest = jnp.maximum(former[member], latter[member])
-        summed = former[member + 1] * jnp.exp(former[member] - highest) + latter[
-            member + 1
-        ] * jnp.exp(latter[member] - highest)
-        merged = merged + [highest, summed]
-    return tuple(merged)
+        merged += [
+            highest,
+            former[member + 1] * jnp.exp(former[member] - highest)
+            + latter[member + 1] * jnp.exp(latter[member] - highest),
+        ]
+    return merged
+
+
+def totals_body(chips, peers, own_ref, out_ref, held, landed, sends, recvs):
+    ctx, vocab, core, chip, sibling = place()
+    stages = [
+        [(sibling, vocab)],
+        [(ctx, (vocab + far) % peers) for far in range(1, peers)],
+        [(((chip + far) % chips) * 2 + core, vocab) for far in range(1, chips)],
+    ]
+    greet(stages[0] + stages[1] + stages[2])
+    state = [own_ref[member] for member in range(4)]
+    slot, copies = 0, []
+    for stage, devices in enumerate(stages):
+        for member in range(4):
+            held[stage, member] = state[member]
+        begin = slot
+        for device in devices:
+            copies.append(
+                push(held.at[stage], landed.at[slot], sends.at[slot], recvs.at[slot], device)
+            )
+            copies[-1].start()
+            slot += 1
+        for at in range(begin, slot):
+            copies[at].wait_recv()
+            state = combine_pairs(state, [landed[at, member] for member in range(4)])
+    for member in range(4):
+        out_ref[member] = state[member]
+    for copy in copies:
+        copy.wait_send()
+
+
+def reduce_body(
+    chips, peers, part_ref, out_ref, pair, v_src, v_dst, z_src, z_dst,
+    p_send, p_recv, v_send, v_recv, z_send, z_recv,
+):
+    ctx, vocab, core, chip, sibling = place()
+    width = part_ref.shape[2] // peers
+    greet(
+        [(sibling, vocab)]
+        + [(((chip + far) % chips) * 2 + core, vocab) for far in range(1, chips)]
+        + [(ctx, (vocab + far) % peers) for far in range(1, peers)]
+    )
+    pair_copies, v_copies, z_copies = [], [], []
+    for step in range(chips):
+        owner = (chip + step + 1) % chips
+        pair_copies.append(
+            push(
+                part_ref.at[owner * 2 + 1 - core],
+                pair.at[step],
+                p_send.at[step],
+                p_recv.at[step],
+                (sibling, vocab),
+            )
+        )
+        pair_copies[-1].start()
+
+    def columns(index):
+        return pl.ds(pl.multiple_of(index * width, 128), width)
+
+    for step in range(chips):
+        owner = (chip + step + 1) % chips
+        pair_copies[step].wait_recv()
+        for far in range(1, peers):
+            target = (vocab + far) % peers
+            v_src[step, far - 1] = (
+                part_ref[owner * 2 + core, :, columns(target)] + pair[step, :, columns(target)]
+            ).astype(jnp.bfloat16)
+            v_copies.append(
+                push(
+                    v_src.at[step, far - 1],
+                    v_dst.at[step, far - 1],
+                    v_send.at[step, far - 1],
+                    v_recv.at[step, far - 1],
+                    (ctx, target),
+                )
+            )
+            v_copies[-1].start()
+    for step in range(chips):
+        owner = (chip + step + 1) % chips
+        total = part_ref[owner * 2 + core, :, columns(vocab)] + pair[step, :, columns(vocab)]
+        for far in range(1, peers):
+            v_copies[step * (peers - 1) + far - 1].wait_recv()
+            total = total + v_dst[step, far - 1].astype(jnp.float32)
+        if step < chips - 1:
+            z_src[step] = total.astype(jnp.bfloat16)
+            z_copies.append(
+                push(
+                    z_src.at[step],
+                    z_dst.at[step],
+                    z_send.at[step],
+                    z_recv.at[step],
+                    (owner * 2 + core, vocab),
+                )
+            )
+            z_copies[-1].start()
+    for step in range(chips - 1):
+        z_copies[step].wait_recv()
+        total = total + z_dst[step].astype(jnp.float32)
+    out_ref[...] = total
+    for copy in pair_copies + v_copies + z_copies:
+        copy.wait_send()
 
 
 def local_totals(logits):
@@ -83,6 +366,9 @@
     local_groups = w_key.shape[1] // head_dim
     group_size = local_heads // local_groups
     ctx_count = lax.axis_size("ctx")
+    chips = ctx_count // 2
+    peers = lax.axis_size("vocab")
+    bf16, f32, dma = jnp.bfloat16, jnp.float32, pltpu.SemaphoreType.DMA
     half_rows = row_count // 2
     stretch_ids = jnp.arange(stretch_order.shape[0], dtype=jnp.int32)
     rollout_ends = jnp.cumsum(rollout_lengths)
@@ -111,12 +397,16 @@
     keys = rotate(keys, query_pos).astype(jnp.bfloat16).reshape(row_count, local_groups * head_dim)
     values = jnp.dot(normed, w_value, preferred_element_type=jnp.float32).astype(jnp.bfloat16)
     score_scale = head_dim ** (-0.5)
-    pieces = (
-        lax.all_gather(keys, "ctx", axis=0, tiled=True),
-        lax.all_gather(values, "ctx", axis=0, tiled=True),
-    )
-    key_piece = pieces[0].reshape(-1, local_groups, head_dim)
-    value_piece = pieces[1].reshape(-1, local_groups, head_dim)
+    own = jnp.concatenate([keys, values], axis=1)
+    gathered = communicate(
+        functools.partial(gather_context_body, chips),
+        jax.ShapeDtypeStruct((ctx_count,) + own.shape, bf16),
+        (own,),
+        spread_sems(chips, 1),
+        0,
+    ).reshape(-1, own.shape[1])
+    key_piece = gathered[:, : keys.shape[1]].reshape(-1, local_groups, head_dim)
+    value_piece = gathered[:, keys.shape[1] :].reshape(-1, local_groups, head_dim)
     key_count = key_piece.shape[0]
     key_pos, key_roll = locate(jnp.int32(0), key_count)
     allowed = (key_pos[None, :] <= query_pos[:, None]) & (key_roll[None, :] == query_roll[:, None])
@@ -142,11 +432,28 @@
         .reshape(row_count, local_heads * head_dim)
     )
     partial_value = jnp.dot(attended, w_out, preferred_element_type=jnp.float32)
-    mixed = hidden_in.astype(jnp.float32) + lax.psum(partial_value, "vocab")
-    final = rms_scale(mixed, final_gain).astype(jnp.bfloat16)
+    width = hidden_in.shape[1]
+    share = row_count // peers
+    final = communicate(
+        functools.partial(mix_and_gather_body, chips, peers),
+        jax.ShapeDtypeStruct((ctx_count, peers, share, width), bf16),
+        (
+            partial_value.reshape(peers, share, width),
+            hidden_in.reshape(peers, share, width),
+            final_gain.reshape(1, width),
+        ),
+        [
+            pltpu.VMEM((peers - 1, share, width), bf16),
+            pltpu.VMEM((peers - 1, share, width), bf16),
+            dma((peers - 1,)),
+            dma((peers - 1,)),
+        ]
+        + spread_sems(chips, peers),
+        1,
+    )
     word_count = teacher_head.shape[0]
     pieces = (
-        lax.all_gather(final, "ctx", axis=0, tiled=True),
+        final.reshape(-1, width),
         lax.all_gather(draft_rows, "ctx", axis=0, tiled=True),
     )
     teacher_part = jnp.einsum(
@@ -155,9 +462,21 @@
     draft_part = jnp.einsum("nd,wd->nw", pieces[1], draft_head, preferred_element_type=jnp.float32)
     teacher_max, teacher_sum = local_totals(teacher_part)
     draft_max, draft_sum = local_totals(draft_part)
-    totals = joined(
-        (teacher_max, teacher_sum, draft_max, draft_sum), ("ctx", "vocab"), combine_pairs
-    )
+    tokens = teacher_max.shape[0]
+    stats = jnp.stack([teacher_max, teacher_sum, draft_max, draft_sum]).reshape(4, -1, 128)
+    hops = 1 + (peers - 1) + (chips - 1)
+    totals = communicate(
+        functools.partial(totals_body, chips, peers),
+        jax.ShapeDtypeStruct(stats.shape, f32),
+        (stats,),
+        [
+            pltpu.VMEM((3,) + stats.shape, f32),
+            pltpu.VMEM((hops,) + stats.shape, f32),
+            dma((hops,)),
+            dma((hops,)),
+        ],
+        2,
+    ).reshape(4, tokens)
     teacher_probs = jnp.exp(teacher_part - totals[0][:, None]) / totals[1][:, None]
     draft_probs = jnp.exp(draft_part - totals[2][:, None]) / totals[3][:, None]
     word_start = (lax.axis_index("vocab") * ctx_count + lax.axis_index("ctx")) * word_count
@@ -166,13 +485,28 @@
         target_ids[:, None] == word_ids[None, :], MIXING, 0.0
     )
     delta = (draft_probs - soft).astype(jnp.bfloat16)
-    reduced = lax.psum_scatter(
-        jnp.dot(delta, draft_head, preferred_element_type=jnp.float32),
-        "ctx",
-        scatter_dimension=0,
-        tiled=True,
-    )
-    return lax.psum_scatter(reduced, "vocab", scatter_dimension=1, tiled=True)
+    grads = jnp.dot(delta, draft_head, preferred_element_type=jnp.float32)
+    features = grads.shape[1]
+    slice_width = features // peers
+    return communicate(
+        functools.partial(reduce_body, chips, peers),
+        jax.ShapeDtypeStruct((row_count, slice_width), f32),
+        (grads.reshape(ctx_count, row_count, features),),
+        [
+            pltpu.VMEM((chips, row_count, features), f32),
+            pltpu.VMEM((chips, peers - 1, row_count, slice_width), bf16),
+            pltpu.VMEM((chips, peers - 1, row_count, slice_width), bf16),
+            pltpu.VMEM((chips - 1, row_count, slice_width), bf16),
+            pltpu.VMEM((chips - 1, row_count, slice_width), bf16),
+            dma((chips,)),
+            dma((chips,)),
+            dma((chips, peers - 1)),
+            dma((chips, peers - 1)),
+            dma((chips - 1,)),
+            dma((chips - 1,)),
+        ],
+        3,
+    )
 
 
 def solution(mesh):

time: 592 us -> 257 us (0.43)
  blocking collectives: 295 us -> 0 us
  waiting for transfers between devices: 184 us -> 0.73 us
  Pallas kernels: 0 us -> 151 us
  other arithmetic: 19.9 us -> 9.13 us
    all_gather x6 -> x0, blocking collectives: 295 us -> none  [the longest x4 265 us: joined(): gathered = jax.tree.map(lambda a: lax.all_gather(a, axis), part)]
    pallas_call x0 -> x4, Pallas kernels: none -> 151 us  [communicate(): pl.pallas_call(body, out_shape=out_shape, in_specs=[pl.BlockSpec(memory_s...]
    reduce_scatter x2 -> x0, waiting for transfers between devices: 114 us -> none  [the longest x1 87.5 us: on_device(): lax.psum_scatter(jnp.dot(delta, draft_head, preferred_element_type=jnp.fl...]
    psum x1 -> x0, waiting for transfers between devices: 69.2 us -> none  [on_device(): mixed = hidden_in.astype(jnp.float32) + lax.psum(partial_value, 'vocab')]
    reduce_sum x2, other arithmetic: 9.29 us -> 2.5 us  [local_totals(): return (highest, jnp.sum(jnp.exp(logits - highest[:, None]), axis=1))]
  transfers between devices with their start and end apart: 5 -> 1, of which waited for: 3 -> 0; matrix products, arithmetic and copies ran while one was open for 4% -> 19% of each run, Pallas kernels for 0% -> 39%
where the time goes in v1:
time: 257 us; the launch traced here: 256 us
  Pallas kernels  151 us (59%)
  matrix products  71.8 us (28%)
  between operations  13.7 us (5%)
  local copies, waits for them, and re-layouts  9.86 us (4%)
  other arithmetic  9.13 us (4%)
    pallas_call x4, Pallas kernels, communicate(): pl.pallas_call(body, out_shape=out_shape, in_specs=[pl.BlockSpec(memory_s...  151 us
    dot_general x1, matrix products, on_device(): jnp.einsum('nd,wd->nw', pieces[0], teacher_head, preferred_element_type=j...  23.3 us
    dot_general x1, matrix products, on_device(): grads = jnp.dot(delta, draft_head, preferred_element_type=jnp.float32)  19 us
    dot_general x1, matrix products, on_device(): jnp.einsum('nd,wd->nw', pieces[1], draft_head, preferred_element_type=jnp...  12.7 us
    unnamed x22, local copies, waits for them, and re-layouts  7.18 us
    dot_general x1, matrix products, on_device(): partial_value = jnp.dot(attended, w_out, preferred_element_type=jnp.float32)  6.1 us
  transfers between devices with their start and end apart: 1, of which 0 were waited for; matrix products, arithmetic and copies ran while one was open for 19% of the time, Pallas kernels for 39%

profile of v1, /device:TPU:0, one launch (start us, length us, event | category | flops | bytes accessed | tf_op | source)
XLA Modules:
  0.0 256.1 jit_solution(339879340124722218)
XLA Ops:
  6.5 0.0 copy-start
  6.5 0.0 copy-start.2
  6.5 0.0 copy-start.5
  6.5 0.0 all-gather.2.cloned.1.call-start
  6.5 0.7 all-gather.2.cloned.1.call-update
  7.3 1.7 fusion.6
  9.0 0.7 select_reduce_fusion.1
  9.8 0.0 copy-done
  9.8 1.7 convolution_convert_fusion
  11.5 0.0 copy-done.2
  11.5 0.0 copy-done.5
  11.5 2.1 fusion.42
  13.6 0.1 reshape.286
  13.7 0.3 multiply_cosine_fusion
  14.0 0.3 subtract_convert_fusion.3
  14.3 0.2 pad_maximum_fusion.1
  14.5 4.7 %convolution_bitcast_fusion = f32[16,8,8,128]{3,1,2,0:T(8,128)S(1)} fusion(bf16[4096,1024]{1,0:T(8,128)(2,1)} %param.15, bf16[128,4096]{1,0:T(8,128)(2,1)S(1)} %copy-done.2, f32[4096]{0:T(1024)S(1)} %copy-done.5, f32[128]{0:T(128)S(1)} %add_rsqrt_fusion), kind=kOutput, calls=%fused_computation.19 | convolution fusion | flops 1075838976 | bytes 9978368 | tf_op jit(solution)/shard_map/dot_general | solution.py:386
  19.2 0.1 copy.40
  19.3 0.0 copy-start.8
  19.3 0.0 copy-start.6
  19.3 0.3 subtract_convert_fusion.2
  19.6 0.7 pad_maximum_fusion.own_ref
  20.3 30.0 %shard_map.127 = bf16[8,128,512]{2,1,0:T(8,128)(2,1)} custom-call(bf16[128,512]{1,0:T(8,128)(2,1)} %pad_maximum_fusion.own_ref), custom_call_target="tpu_custom_call" | custom-call | tf_op jit(solution)/shard_map/pallas_call | solution.py:165
  50.3 1.3 fusion.46
  51.7 0.2 copy.38
  51.9 0.2 copy.26
  52.1 0.0 copy-done.8
  52.1 0.2 reduce-window.8
  52.3 0.1 convert_reduce_fusion.1
  52.4 0.0 copy-done.6
  52.4 0.1 select_reduce_fusion
  52.5 0.1 convert_reduce_fusion
  52.6 0.3 compare_and_fusion
  52.9 1.0 fusion.3
  53.9 1.0 fusion.4
  54.9 1.2 fusion.18
  56.1 0.2 copy.32
  56.3 0.2 dot_general.35
  56.5 6.1 %fusion.part_ref = f32[4,32,4096]{2,1,0:T(8,128)} fusion(bf16[4,32,1024]{2,1,0:T(8,128)(2,1)S(1)} %dot_general.35, bf16[1024,4096]{1,0:T(8,128)(2,1)} %param.18), kind=kOutput, calls=%fused_computation | convolution fusion | flops 1073741824 | bytes 10747904 | tf_op jit(solution)/shard_map/dot_general | solution.py:434
  62.6 70.4 %shard_map.128 = bf16[8,4,32,4096]{3,2,1,0:T(8,128)(2,1)} custom-call(f32[4,32,4096]{2,1,0:T(8,128)} %fusion.part_ref, bf16[4,32,4096]{2,1,0:T(8,128)(2,1)} %bitcast.75, f32[1,4096]{1,0:T(1,128)} %bitcast.90), custom_call_target="tpu_custom_call" | custom-call | tf_op jit(solution)/shard_map/pallas_call | solution.py:165
  133.0 23.3 %fusion.48 = (f32[1024]{0:T(1024)S(1)}, f32[1024,2048]{1,0:T(8,128)S(1)}) fusion(bf16[1024,4096]{1,0:T(8,128)(2,1)} %bitcast.77, bf16[2048,4096]{1,0:T(8,128)(2,1)} %param.20), kind=kOutput, calls=%fused_computation.81 | convolution fusion | flops 17181966336 | bytes 33558528 | tf_op jit(solution)/shard_map/nd,wd->nw/dot_general | solution.py:459
  156.3 0.0 copy-start.3
  156.3 3.2 %copy-done.3 = f32[1024,2048]{1,0:T(8,128)} copy-done((f32[1024,2048]{1,0:T(8,128)}, f32[1024,2048]{1,0:T(8,128)S(1)}, u32[]{:S(2)}) %copy-start.3) | copy-done | bytes 8388632
  159.5 1.3 exponential_reduce_fusion.1
  160.8 0.0 all-gather.2.cloned.1.call-done
  160.8 12.7 %fusion.47 = (f32[1024]{0:T(1024)S(1)}, f32[1024,2048]{1,0:T(8,128)S(1)}) fusion(bf16[1024,2048]{1,0:T(8,128)(2,1)} %all-gather.2.cloned.1.call-done, bf16[2048,2048]{1,0:T(8,128)(2,1)} %param.22), kind=kOutput, calls=%fused_computation.80 | convolution fusion | flops 8592030720 | bytes 20975616 | tf_op jit(solution)/shard_map/nd,wd->nw/dot_general | solution.py:462
  173.6 0.0 copy-start.4
  173.6 0.0 copy-start.7
  173.6 1.2 exponential_reduce_fusion
  174.8 1.9 copy-done.4
  176.8 0.6 pad_maximum_fusion.2.own_ref
  177.4 17.6 %shard_map.129 = f32[4,8,128]{2,1,0:T(8,128)} custom-call(f32[4,8,128]{2,1,0:T(8,128)} %pad_maximum_fusion.2.own_ref), custom_call_target="tpu_custom_call" | custom-call | tf_op jit(solution)/shard_map/pallas_call | solution.py:165
  195.0 0.7 slice_bitcast_fusion.3
  195.7 0.0 copy-done.7
  195.7 19.0 %fusion.2 = f32[1024,2048]{1,0:T(8,128)} fusion(bf16[2048,2048]{1,0:T(8,128)(2,1)} %param.22, f32[1024,2048]{1,0:T(8,128)} %copy-done.3, f32[1024,2048]{1,0:T(8,128)} %copy-done.4, s32[2048]{0:T(1024)S(1)} %iota_add_fusion, f32[1024]{0:T(1024)S(1)} %get-tuple-element.14, f32[1024]{0:T(1024)S(1)} %get-tuple-element.15, f32[1024]{0:T(1024)S(1)} %get-tuple-element.16, ...), kind=kOutput, calls=%fused_computation.7 | convolution fusion | flops 8610906112 | bytes 33583104 | tf_op jit(solution)/shard_map/dot_general | solution.py:488
  214.7 0.0 copy-start.1
  214.7 32.9 %shard_map.130 = f32[128,512]{1,0:T(8,128)} custom-call(f32[8,128,2048]{2,1,0:T(8,128)} %bitcast.76), custom_call_target="tpu_custom_call" | custom-call | tf_op jit(solution)/shard_map/pallas_call | solution.py:165
  247.6 1.7 copy.44
  249.3 0.0 copy-done.1
  (11 shorter events, 0.1 us)
Async XLA Ops:
  6.5 3.3 %copy-start = (bf16[4096,256]{1,0:T(8,128)(2,1)S(1)}, bf16[4096,256]{1,0:T(8,128)(2,1)}, u32[]{:S(2)}) copy-start(bf16[4096,256]{1,0:T(8,128)(2,1)} %param.17) | copy-start | bytes 6291460
  6.5 5.0 %copy-start.2 = (bf16[128,4096]{1,0:T(8,128)(2,1)S(1)}, bf16[128,4096]{1,0:T(8,128)(2,1)}, u32[]{:S(2)}) copy-start(bf16[128,4096]{1,0:T(8,128)(2,1)} %param.13) | copy-start | bytes 3145732
  6.5 5.0 %copy-start.5 = (f32[4096]{0:T(1024)S(1)}, f32[4096]{0:T(1024)}, u32[]{:S(2)}) copy-start(f32[4096]{0:T(1024)} %param.14) | copy-start | bytes 49156
  6.5 154.3 %all-gather.2.cloned.1.call-start = ((), (), s32[]{:S(2)}) async-start(), calls=%async_computation | async-start | bytes 4718592 | tf_op jit(solution)/shard_map/all_gather | solution.py:457
  19.3 32.8 %copy-start.8 = (s32[4]{0:T(128)S(1)}, s32[4]{0:T(128)}, u32[]{:S(2)}) copy-start(s32[4]{0:T(128)} %param.24) | copy-start | bytes 52
  19.3 33.1 %copy-start.6 = (s32[16]{0:T(128)S(1)}, s32[16]{0:T(128)}, u32[]{:S(2)}) copy-start(s32[16]{0:T(128)} %param.25) | copy-start | bytes 196
  156.3 3.2 %copy-start.3 = (f32[1024,2048]{1,0:T(8,128)}, f32[1024,2048]{1,0:T(8,128)S(1)}, u32[]{:S(2)}) copy-start(f32[1024,2048]{1,0:T(8,128)S(1)} %get-tuple-element.24) | copy-start | bytes 25165828
  173.6 3.2 %copy-start.4 = (f32[1024,2048]{1,0:T(8,128)}, f32[1024,2048]{1,0:T(8,128)S(1)}, u32[]{:S(2)}) copy-start(f32[1024,2048]{1,0:T(8,128)S(1)} %get-tuple-element.22) | copy-start | bytes 25165828
  173.6 22.1 %copy-start.7 = (s32[1024]{0:T(1024)S(1)}, s32[1024]{0:T(1024)}, u32[]{:S(2)}) copy-start(s32[1024]{0:T(1024)} %param.23) | copy-start | bytes 12292
  214.7 34.6 %copy-start.1 = (bf16[4096,256]{1,0:T(8,128)(2,1)S(1)}, bf16[4096,256]{1,0:T(8,128)(2,1)}, u32[]{:S(2)}) copy-start(bf16[4096,256]{1,0:T(8,128)(2,1)} %param.17) | copy-start | bytes 6291460
Sparse Core Ops, SparseCore 0:
  9.0 60.9 all-gather.1

commit v2 on v1

v2 whole, which is shorter than its diff:
```python
import functools

import jax
import jax.numpy as jnp
from jax import lax
from jax.experimental import pallas as pl
from jax.experimental.pallas import tpu as pltpu
from jax.sharding import PartitionSpec as P

HEAD_DIM = 128


EPSILON = 1e-05
ROPE_BASE = 500000.0
MIXING = 0.5
NEGATIVE = -1e30


def rms_scale(values, gain):
    mean_square = jnp.mean(values * values, axis=-1, keepdims=True)
    return values * lax.rsqrt(mean_square + EPSILON) * gain


def rotate(vectors, positions):
    half_dim = vectors.shape[-1] // 2
    exponents = jnp.arange(half_dim, dtype=jnp.float32) * (2.0 / vectors.shape[-1])
    frequencies = jnp.power(ROPE_BASE, -exponents)
    angles = positions.astype(jnp.float32)[:, None] * frequencies[None, :]
    cosine_values = jnp.cos(angles)[:, None, :]
    sine_values = jnp.sin(angles)[:, None, :]
    leading = vectors[..., :half_dim]
    trailing = vectors[..., half_dim:]
    return jnp.concatenate(
        [
            leading * cosine_values - trailing * sine_values,
            trailing * cosine_values + leading * sine_values,
        ],
        axis=-1,
    )


MESH = pl.DeviceIdType.MESH
VMEM_LIMIT = 56 * 1024 * 1024


def place():
    ctx = lax.axis_index("ctx")
    core = ctx % 2
    return ctx, lax.axis_index("vocab"), core, ctx // 2, ctx + 1 - 2 * core


def flip(index, mask):
    bit = 1
    while bit <= mask:
        if mask & bit:
            index = index + bit * (1 - 2 * ((index // bit) % 2))
        bit *= 2
    return index


def greet(devices):
    barrier = pltpu.get_barrier_semaphore()
    for device in devices:
        pl.semaphore_signal(barrier, inc=1, device_id=device, device_id_type=MESH)
    pl.semaphore_wait(barrier, len(devices))


def push(source, target, send, recv, device):
    return pltpu.make_async_remote_copy(
        src_ref=source,
        dst_ref=target,
        send_sem=send,
        recv_sem=recv,
        device_id=device,
        device_id_type=MESH,
    )


class Spread:
    def __init__(self, chips, peers, block, sems):
        self.chips, self.peers, self.block, self.sems = chips, peers, block, sems
        self.bits = [1 << i for i in range(peers.bit_length() - 1)]
        self.orders = (self.bits, self.bits[::-1])
        self.sent = []

    def piece(self, far, mask, half, other=False):
        ctx, vocab, core, chip, sibling = place()
        source = ((chip - far + self.chips) % self.chips) * 2 + (1 - core if other else core)
        return self.block(source, flip(vocab, mask), half)

    def send(self, piece, send, recv, device):
        self.sent.append(push(piece, piece, send, recv, device))
        self.sent[-1].start()

    def arrive(self, piece, sem):
        ctx, vocab, core, chip, sibling = place()
        push(piece, piece, sem, sem, (sibling, vocab)).wait_recv()

    def hand_on(self, far, mask, half):
        ctx, vocab, core, chip, sibling = place()
        z_send, z_recv, v_send, v_recv, s_send, s_recv = self.sems
        piece = self.piece(far, mask, half)
        order = self.orders[half]
        reached = [i for i, bit in enumerate(order) if mask & bit]
        for i in range(reached[-1] + 1 if reached else 0, len(order)):
            self.send(
                piece,
                v_send.at[far, half, mask, i],
                v_recv.at[far, half, mask | order[i]],
                (ctx, flip(vocab, order[i])),
            )
        self.send(
            piece, s_send.at[far, half, mask], s_recv.at[far, half, mask], (sibling, vocab)
        )

    def start(self):
        ctx, vocab, core, chip, sibling = place()
        z_send, z_recv = self.sems[:2]
        for half in (0, 1):
            for far in range(1, self.chips):
                self.send(
                    self.piece(0, 0, half),
                    z_send.at[far, half],
                    z_recv.at[far, half],
                    (((chip + far) % self.chips) * 2 + core, vocab),
                )
            self.hand_on(0, 0, half)

    def steps(self):
        return range(1, self.chips + len(self.bits))

    def step(self, step):
        z_recv, v_recv = self.sems[1], self.sems[3]
        for level in range(0, len(self.bits) + 1):
            far = step - level
            if not 0 <= far < self.chips or (far == 0 and level == 0):
                continue
            for half in (0, 1):
                for mask in [m for m in range(self.peers) if bin(m).count("1") == level]:
                    sem = v_recv.at[far, half, mask] if mask else z_recv.at[far, half]
                    self.arrive(self.piece(far, mask, half), sem)
                    self.hand_on(far, mask, half)

    def collect(self, far):
        for half in (0, 1):
            for mask in range(self.peers):
                self.arrive(self.piece(far, mask, half, True), self.sems[5].at[far, half, mask])

    def finish(self):
        for copy in self.sent:
            copy.wait_send()


def spread_sems(chips, peers):
    dma = pltpu.SemaphoreType.DMA
    depth = max(1, peers.bit_length() - 1)
    return [
        dma((chips, 2)),
        dma((chips, 2)),
        dma((chips, 2, peers, depth)),
        dma((chips, 2, peers)),
        dma((chips, 2, peers)),
        dma((chips, 2, peers)),
    ]


def communicate(body, out_shape, operands, scratch, collective, in_kinds=None, out_kinds=None):
    in_kinds = in_kinds or [pltpu.VMEM] * len(operands)
    out_kinds = out_kinds or [pltpu.VMEM] * len(out_shape)
    return pl.pallas_call(
        body,
        out_shape=out_shape,
        in_specs=[pl.BlockSpec(memory_space=kind) for kind in in_kinds],
        out_specs=[pl.BlockSpec(memory_space=kind) for kind in out_kinds],
        scratch_shapes=scratch,
        compiler_params=pltpu.CompilerParams(
            collective_id=collective, has_side_effects=True, vmem_limit_bytes=VMEM_LIMIT
        ),
    )(*operands)


def gather_context_body(chips, own_ref, out_ref, *sems):
    ctx, vocab, core, chip, sibling = place()
    width = own_ref.shape[1] // 2
    greet(
        [(sibling, vocab)]
        + [(((chip + far) % chips) * 2 + core, vocab) for far in range(1, chips)]
    )
    out_ref[ctx] = own_ref[...]
    blocks = Spread(
        chips, 1, lambda c, v, half: out_ref.at[c, :, half * width : (half + 1) * width], sems
    )
    blocks.start()
    for step in blocks.steps():
        blocks.step(step)
    for far in range(chips):
        blocks.collect(far)
    blocks.finish()


def combine_pairs(former, latter):
    merged = []
    for member in (0, 2):
        highest = jnp.maximum(former[member], latter[member])
        merged += [
            highest,
            former[member + 1] * jnp.exp(former[member] - highest)
            + latter[member + 1] * jnp.exp(latter[member] - highest),
        ]
    return merged


def halves(rows):
    width = rows.shape[-1] // 2
    return lambda c, v, half: rows.at[c, v, :, half * width : (half + 1) * width]


def logits_body(
    chips, peers, part_ref, hidden_ref, gain_ref, draft_ref, t_head, d_head,
    t_out, d_out, totals_ref,
    final_all, draft_all, t_words, d_words, slots, columns, held, landed, send_buf, recv_buf,
    load_sem, store_sem, r_send, r_recv, x_send, x_recv, *sems,
):
    ctx, vocab, core, chip, sibling = place()
    stages = [
        [(sibling, vocab)],
        [(ctx, (vocab + far) % peers) for far in range(1, peers)],
        [(((chip + far) % chips) * 2 + core, vocab) for far in range(1, chips)],
    ]
    loads = [
        pltpu.make_async_copy(d_head, d_words, load_sem.at[0]),
        pltpu.make_async_copy(t_head, t_words, load_sem.at[1]),
    ]
    for load in loads:
        load.start()
    greet(stages[0] + stages[1] + stages[2])
    copies = []
    for far in range(1, peers):
        owner = (vocab + far) % peers
        send_buf[far - 1] = part_ref[owner].astype(jnp.bfloat16)
        copies.append(
            push(
                send_buf.at[far - 1],
                recv_buf.at[far - 1],
                r_send.at[far - 1],
                r_recv.at[far - 1],
                (ctx, owner),
            )
        )
        copies[-1].start()
    draft_all[ctx, vocab] = draft_ref[vocab]
    draft = Spread(chips, peers, halves(draft_all), sems[:6])
    teacher = Spread(chips, peers, halves(final_all), sems[6:])
    draft.start()
    for step in range(1, chips):
        draft.step(step)
    for copy in copies:
        copy.wait_recv()
    mixed = hidden_ref[vocab].astype(jnp.float32) + part_ref[vocab]
    for far in range(1, peers):
        mixed = mixed + recv_buf[far - 1].astype(jnp.float32)
    final_all[ctx, vocab] = rms_scale(mixed, gain_ref[...]).astype(jnp.bfloat16)
    teacher.start()
    for step in draft.steps():
        if step >= chips:
            draft.step(step)

    rows, words = slots.shape[1], slots.shape[2]
    tile = min(words, 512)
    group = 32
    held[...] = jnp.zeros_like(held)
    stores = []

    def multiply(blocks, source_ref, head_ref, out_ref, member, far):
        count = len(stores)
        slot = count % 2
        blocks.collect(far)
        owner = (chip - far + chips) % chips
        if count >= 2:
            stores[count - 2].wait()

        def over_words(i, carry):
            at = pl.ds(pl.multiple_of(i * tile, tile), tile)
            left = source_ref[pl.ds(owner * 2, 2)].reshape(rows, source_ref.shape[3])
            slots[slot, :, at] = lax.dot_general(
                left,
                head_ref[at, :],
                (((1,), (1,)), ((), ())),
                preferred_element_type=jnp.float32,
            )
            return carry

        lax.fori_loop(0, words // tile, over_words, 0)
        store = pltpu.make_async_copy(
            slots.at[slot],
            out_ref.at[pl.ds(pl.multiple_of(owner * rows, rows), rows)],
            store_sem.at[count],
        )
        store.start()
        stores.append(store)

        def over_rows(i, carry):
            at = pl.ds(pl.multiple_of(i * group, group), group)
            values = slots[slot, at, :]
            highest = jnp.max(values, axis=1, keepdims=True)
            summed = jnp.sum(jnp.exp(values - highest), axis=1, keepdims=True)
            columns[0, at, :] = jnp.broadcast_to(highest, (group, 128))
            columns[1, at, :] = jnp.broadcast_to(summed, (group, 128))
            return carry

        lax.fori_loop(0, rows // group, over_rows, 0)
        lanes = pl.ds(pl.multiple_of(owner * rows, rows), rows)
        for which in (0, 1):
            held[0, member + which : member + which + 1, lanes] = jnp.transpose(columns[which])[:1]

    for load in loads:
        load.wait()
    done = [0, 0]
    for step in teacher.steps():
        teacher.step(step)
        if done[0] < chips:
            multiply(draft, draft_all, d_words, d_out, 2, done[0])
            done[0] += 1
        if step > len(teacher.bits):
            multiply(teacher, final_all, t_words, t_out, 0, done[1])
            done[1] += 1
    for far in range(done[0], chips):
        multiply(draft, draft_all, d_words, d_out, 2, far)
    for far in range(done[1], chips):
        multiply(teacher, final_all, t_words, t_out, 0, far)

    state = [held[0, member : member + 1] for member in range(4)]
    slot, x_copies = 0, []
    for stage, devices in enumerate(stages):
        if stage:
            for member in range(4):
                held[stage, member : member + 1] = state[member]
        begin = slot
        for device in devices:
            x_copies.append(
                push(held.at[stage], landed.at[slot], x_send.at[slot], x_recv.at[slot], device)
            )
            x_copies[-1].start()
            slot += 1
        for at in range(begin, slot):
            x_copies[at].wait_recv()
            state = combine_pairs(
                state, [landed[at, member : member + 1] for member in range(4)]
            )
    totals_ref[...] = jnp.zeros_like(totals_ref)
    for member in range(4):
        totals_ref[member : member + 1] = state[member]
    for copy in copies + x_copies:
        copy.wait_send()
    draft.finish()
    teacher.finish()
    for store in stores[-2:]:
        store.wait()


def gradient_body(
    chips, peers, totals_ref, target_ref, t_logits, d_logits, d_head, out_ref,
    d_words, t_rows, d_rows, delta, grads, pair, v_src, v_dst, z_src, z_dst,
    load_sem, t_sem, d_sem, p_send, p_recv, v_send, v_recv, z_send, z_recv,
):
    ctx, vocab, core, chip, sibling = place()
    rows, words = t_rows.shape[1], t_rows.shape[2]
    half_rows = rows // 2
    width = out_ref.shape[1]
    features = d_words.shape[1]
    tile = min(features, 512)
    group = 32
    word_start = (vocab * chips * 2 + ctx) * words

    def block_rows(step):
        owner = (chip + step + 1) % chips
        return pl.ds(pl.multiple_of(owner * rows, rows), rows)

    def fetch(step):
        slot = step % 2
        pairs = [
            pltpu.make_async_copy(
                t_logits.at[block_rows(step)], t_rows.at[slot], t_sem.at[step]
            ),
            pltpu.make_async_copy(
                d_logits.at[block_rows(step)], d_rows.at[slot], d_sem.at[step]
            ),
        ]
        for item in pairs:
            item.start()
        return pairs

    fetched = [fetch(0)]
    load = pltpu.make_async_copy(d_head, d_words, load_sem.at[0])
    load.start()
    greet(
        [(sibling, vocab)]
        + [(((chip + far) % chips) * 2 + core, vocab) for far in range(1, chips)]
        + [(ctx, (vocab + far) % peers) for far in range(1, peers)]
    )
    pair_copies, v_copies, z_copies = [], {}, []

    def column(values):
        return jnp.transpose(jnp.broadcast_to(values, (128, rows)))[:, :1]

    def features_of(index):
        return pl.ds(pl.multiple_of(index * width, 128), width)

    def make(step):
        slot = step % 2
        for item in fetched[step]:
            item.wait()
        if step + 1 < chips:
            fetched.append(fetch(step + 1))
        lanes = block_rows(step)
        t_high = column(totals_ref[0:1, lanes])
        t_scale = column((1.0 - MIXING) / totals_ref[1:2, lanes])
        d_high = column(totals_ref[2:3, lanes])
        d_scale = column(1.0 / totals_ref[3:4, lanes])
        target = column(target_ref[0:1, lanes]).astype(jnp.int32)
        ids = word_start + lax.broadcasted_iota(jnp.int32, (group, words), 1)
        for begin in range(0, rows, group):
            at = slice(begin, begin + group)
            soft = jnp.exp(t_rows[slot, at, :] - t_high[at]) * t_scale[at] + jnp.where(
                target[at] == ids, MIXING, 0.0
            )
            drafted = jnp.exp(d_rows[slot, at, :] - d_high[at]) * d_scale[at]
            delta[at, :] = (drafted - soft).astype(jnp.bfloat16)
        if step == 0:
            load.wait()

        def over_features(i, carry):
            at = pl.ds(pl.multiple_of(i * tile, tile), tile)
            product = jnp.dot(delta[...], d_words[:, at], preferred_element_type=jnp.float32)
            grads[step, 0, :, at] = product[:half_rows]
            grads[step, 1, :, at] = product[half_rows:]
            return carry

        lax.fori_loop(0, features // tile, over_features, 0)
        pair_copies.append(
            push(
                grads.at[step, 1 - core],
                pair.at[step],
                p_send.at[step],
                p_recv.at[step],
                (sibling, vocab),
            )
        )
        pair_copies[-1].start()

    def over_vocab(step):
        pair_copies[step].wait_recv()
        for far in range(1, peers):
            at = features_of((vocab + far) % peers)
            v_src[step, far - 1] = (grads[step, core, :, at] + pair[step, :, at]).astype(
                jnp.bfloat16
            )
            v_copies[step, far] = push(
                v_src.at[step, far - 1],
                v_dst.at[step, far - 1],
                v_send.at[step, far - 1],
                v_recv.at[step, far - 1],
                (ctx, (vocab + far) % peers),
            )
            v_copies[step, far].start()

    def over_chips(step):
        at = features_of(vocab)
        total = grads[step, core, :, at] + pair[step, :, at]
        for far in range(1, peers):
            v_copies[step, far].wait_recv()
            total = total + v_dst[step, far - 1].astype(jnp.float32)
        if step == chips - 1:
            return total
        z_src[step] = total.astype(jnp.bfloat16)
        owner = (chip + step + 1) % chips
        z_copies.append(
            push(
                z_src.at[step],
                z_dst.at[step],
                z_send.at[step],
                z_recv.at[step],
                (owner * 2 + core, vocab),
            )
        )
        z_copies[-1].start()
        return total

    for step in range(chips + 2):
        if step < chips:
            make(step)
        if 0 <= step - 1 < chips:
            over_vocab(step - 1)
        if 0 <= step - 2 < chips:
            total = over_chips(step - 2)
    for step in range(chips - 1):
        z_copies[step].wait_recv()
        total = total + z_dst[step].astype(jnp.float32)
    out_ref[...] = total
    for copy in pair_copies + list(v_copies.values()) + z_copies:
        copy.wait_send()


def on_device(
    hidden_in,
    attn_gain,
    w_query,
    w_key,
    w_value,
    w_out,
    final_gain,
    teacher_head,
    draft_rows,
    draft_head,
    target_ids,
    rollout_lengths,
    stretch_order,
):
    row_count = hidden_in.shape[0]
    head_dim = HEAD_DIM
    local_heads = w_query.shape[1] // head_dim
    local_groups = w_key.shape[1] // head_dim
    group_size = local_heads // local_groups
    ctx_count = lax.axis_size("ctx")
    chips = ctx_count // 2
    peers = lax.axis_size("vocab")
    bf16, f32, dma = jnp.bfloat16, jnp.float32, pltpu.SemaphoreType.DMA
    half_rows = row_count // 2
    stretch_ids = jnp.arange(stretch_order.shape[0], dtype=jnp.int32)
    rollout_ends = jnp.cumsum(rollout_lengths)

    def locate(begin_row, span_rows):
        row_ids = begin_row + jnp.arange(span_rows, dtype=jnp.int32)
        stretch_hit = (row_ids // half_rows)[:, None] == stretch_ids[None, :]
        stretch_start = jnp.sum(jnp.where(stretch_hit, stretch_order[None, :], 0), axis=1)
        positions = stretch_start * half_rows + row_ids % half_rows
        rollouts = jnp.sum((positions[:, None] >= rollout_ends[None, :]).astype(jnp.int32), axis=1)
        return (positions, rollouts)

    query_pos, query_roll = locate(lax.axis_index("ctx") * row_count, row_count)
    normed = rms_scale(hidden_in.astype(jnp.float32), attn_gain).astype(jnp.bfloat16)
    queries = jnp.dot(normed, w_query, preferred_element_type=jnp.float32).reshape(
        row_count, local_heads, head_dim
    )
    queries = (
        rotate(queries, query_pos)
        .astype(jnp.bfloat16)
        .reshape(row_count, local_groups, group_size, head_dim)
    )
    keys = jnp.dot(normed, w_key, preferred_element_type=jnp.float32).reshape(
        row_count, local_groups, head_dim
    )
    keys = rotate(keys, query_pos).astype(jnp.bfloat16).reshape(row_count, local_groups * head_dim)
    values = jnp.dot(normed, w_value, preferred_element_type=jnp.float32).astype(jnp.bfloat16)
    score_scale = head_dim ** (-0.5)
    own = jnp.concatenate([keys, values], axis=1)
    gathered = communicate(
        functools.partial(gather_context_body, chips),
        [jax.ShapeDtypeStruct((ctx_count,) + own.shape, bf16)],
        (own,),
        spread_sems(chips, 1),
        0,
    )[0].reshape(-1, own.shape[1])
    key_piece = gathered[:, : keys.shape[1]].reshape(-1, local_groups, head_dim)
    value_piece = gathered[:, keys.shape[1] :].reshape(-1, local_groups, head_dim)
    key_count = key_piece.shape[0]
    key_pos, key_roll = locate(jnp.int32(0), key_count)
    allowed = (key_pos[None, :] <= query_pos[:, None]) & (key_roll[None, :] == query_roll[:, None])
    running_max = jnp.full((row_count, local_groups, group_size), NEGATIVE, jnp.float32)
    visible = allowed[:, None, None, :]
    scores = (
        jnp.einsum("tkgd,nkd->tkgn", queries, key_piece, preferred_element_type=jnp.float32)
        * score_scale
    )
    scores = jnp.where(visible, scores, NEGATIVE)
    new_max = jnp.maximum(running_max, jnp.max(scores, axis=-1))
    weights = jnp.where(visible, jnp.exp(scores - new_max[..., None]), 0.0)
    new_sum = jnp.sum(weights, axis=-1)
    new_weighted = jnp.einsum(
        "tkgn,nkd->tkgd",
        weights.astype(jnp.bfloat16),
        value_piece,
        preferred_element_type=jnp.float32,
    )
    attended = (
        (new_weighted / new_sum[..., None])
        .astype(jnp.bfloat16)
        .reshape(row_count, local_heads * head_dim)
    )
    partial_value = jnp.dot(attended, w_out, preferred_element_type=jnp.float32)
    width = hidden_in.shape[1]
    share = row_count // peers
    word_count, features = draft_head.shape
    tokens = row_count * ctx_count
    unit = 2 * row_count
    hops = 1 + (peers - 1) + (chips - 1)
    logits = jax.ShapeDtypeStruct((tokens, word_count), f32)
    teacher_part, draft_part, totals = communicate(
        functools.partial(logits_body, chips, peers),
        [logits, logits, jax.ShapeDtypeStruct((8, tokens), f32)],
        (
            partial_value.reshape(peers, share, width),
            hidden_in.reshape(peers, share, width),
            final_gain.reshape(1, width),
            draft_rows.reshape(peers, share, features),
            teacher_head,
            draft_head,
        ),
        [
            pltpu.VMEM((ctx_count, peers, share, width), bf16),
            pltpu.VMEM((ctx_count, peers, share, features), bf16),
            pltpu.VMEM(teacher_head.shape, bf16),
            pltpu.VMEM(draft_head.shape, bf16),
            pltpu.VMEM((2, unit, word_count), f32),
            pltpu.VMEM((2, unit, 128), f32),
            pltpu.VMEM((3, 8, tokens), f32),
            pltpu.VMEM((hops, 8, tokens), f32),
            pltpu.VMEM((peers - 1, share, width), bf16),
            pltpu.VMEM((peers - 1, share, width), bf16),
            dma((2,)),
            dma((2 * chips,)),
            dma((peers - 1,)),
            dma((peers - 1,)),
            dma((hops,)),
            dma((hops,)),
        ]
        + spread_sems(chips, peers)
        + spread_sems(chips, peers),
        1,
        [pltpu.VMEM] * 4 + [pl.ANY] * 2,
        [pl.ANY, pl.ANY, pltpu.VMEM],
    )
    slice_width = features // peers
    return communicate(
        functools.partial(gradient_body, chips, peers),
        [jax.ShapeDtypeStruct((row_count, slice_width), f32)],
        (
            totals,
            target_ids.astype(f32).reshape(1, tokens),
            teacher_part,
            draft_part,
            draft_head,
        ),
        [
            pltpu.VMEM(draft_head.shape, bf16),
            pltpu.VMEM((2, unit, word_count), f32),
            pltpu.VMEM((2, unit, word_count), f32),
            pltpu.VMEM((unit, word_count), bf16),
            pltpu.VMEM((chips, 2, row_count, features), f32),
            pltpu.VMEM((chips, row_count, features), f32),
            pltpu.VMEM((chips, peers - 1, row_count, slice_width), bf16),
            pltpu.VMEM((chips, peers - 1, row_count, slice_width), bf16),
            pltpu.VMEM((chips - 1, row_count, slice_width), bf16),
            pltpu.VMEM((chips - 1, row_count, slice_width), bf16),
            dma((1,)),
            dma((chips,)),
            dma((chips,)),
            dma((chips,)),
            dma((chips,)),
            dma((chips, peers - 1)),
            dma((chips, peers - 1)),
            dma((chips - 1,)),
            dma((chips - 1,)),
        ],
        2,
        [pltpu.VMEM] * 2 + [pl.ANY] * 3,
    )[0]


def solution(mesh):
    placed = (
        P("ctx", None),
        P(),
        P(None, "vocab"),
        P(None, "vocab"),
        P(None, "vocab"),
        P("vocab", None),
        P(),
        P(("vocab", "ctx"), None),
        P("ctx", None),
        P(("vocab", "ctx"), None),
        P(),
        P(),
        P(),
    )
    return jax.shard_map(
        on_device, mesh=mesh, in_specs=placed, out_specs=P("ctx", "vocab"), check_vma=False
    )
```

time: 257 us -> 210 us (0.82)
  matrix products: 71.8 us -> 18.8 us
  Pallas kernels: 151 us -> 178 us
  between operations: 13.7 us -> 0.27 us
  local copies, waits for them, and re-layouts: 9.86 us -> 6.7 us
  other arithmetic: 9.13 us -> 6.55 us
    dot_general x3 -> x0, matrix products: 55 us -> none  [the longest x1 23.3 us: on_device(): jnp.einsum('nd,wd->nw', pieces[0], teacher_head, preferred_element_type=j...]
    pallas_call x4 -> x3, Pallas kernels: 151 us -> 178 us  [communicate(): pl.pallas_call(body, out_shape=out_shape, in_specs=[pl.BlockSpec(memory_s...]
    unnamed x22, local copies, waits for them, and re-layouts: 7.18 us -> 3.93 us
  transfers between devices with their start and end apart: 1 -> 0, of which waited for: 0 -> 0; matrix products, arithmetic and copies ran while one was open for 19% -> 0% of each run, Pallas kernels for 39% -> 0%
where the time goes in v2:
time: 210 us
  Pallas kernels  178 us (85%)
  matrix products  18.8 us (9%)
  local copies, waits for them, and re-layouts  6.7 us (3%)
  other arithmetic  6.55 us (3%)
    pallas_call x3, Pallas kernels, communicate(): pl.pallas_call(body, out_shape=out_shape, in_specs=[pl.BlockSpec(memory_s...  178 us
    dot_general x1, matrix products, on_device(): partial_value = jnp.dot(attended, w_out, preferred_element_type=jnp.float32)  6 us
    dot_general x1, matrix products, on_device(): jnp.dot(normed, w_query, preferred_element_type=jnp.float32)  4.68 us

profile of v2, /device:TPU:0, one launch (start us, length us, event | category | flops | bytes accessed | tf_op | source)
XLA Modules:
  0.0 210.0 jit_solution(12506879055038625004)
XLA Ops:
  0.0 0.0 copy-start
  0.0 0.0 copy-start.3
  0.0 0.0 copy-start.5
  0.0 0.9 select_reduce_fusion.1
  0.9 0.3 multiply_cosine_fusion
  1.3 1.5 fusion.5
  2.8 0.0 copy-done
  2.8 1.7 fusion.39
  4.5 0.1 reshape.257
  4.6 0.3 subtract_convert_fusion.1
  4.9 0.2 pad_maximum_fusion.1
  5.1 0.0 copy-start.8
  5.1 0.0 copy-start.7
  5.1 0.0 copy-done.3
  5.1 0.0 copy-done.5
  5.1 2.1 convolution_convert_fusion
  7.2 0.7 pad_maximum_fusion.own_ref
  7.9 19.8 %shard_map.127 = bf16[8,128,512]{2,1,0:T(8,128)(2,1)} custom-call(bf16[128,512]{1,0:T(8,128)(2,1)} %pad_maximum_fusion.own_ref), custom_call_target="tpu_custom_call" | custom-call | tf_op jit(solution)/shard_map/pallas_call | solution.py:170
  27.7 2.1 fusion.43
  29.7 0.2 copy.38
  29.9 0.0 copy-done.8
  29.9 0.2 reduce-window.8
  30.1 0.1 convert_reduce_fusion.1
  30.2 0.0 copy-done.7
  30.2 0.1 select_reduce_fusion
  30.3 0.1 convert_reduce_fusion
  30.4 0.3 compare_and_fusion
  30.7 4.7 %convolution_bitcast_fusion = f32[16,8,8,128]{3,1,2,0:T(8,128)S(1)} fusion(bf16[4096,1024]{1,0:T(8,128)(2,1)} %param.15, bf16[128,4096]{1,0:T(8,128)(2,1)S(1)} %copy-done.3, f32[4096]{0:T(1024)S(1)} %copy-done.5, f32[128]{0:T(128)S(1)} %add_rsqrt_fusion), kind=kOutput, calls=%fused_computation.15 | convolution fusion | flops 1075838976 | bytes 9978368 | tf_op jit(solution)/shard_map/dot_general | solution.py:542
  35.4 0.1 copy.40
  35.5 0.3 subtract_convert_fusion
  35.9 0.0 copy-start.4
  35.9 1.0 fusion.2
  36.9 0.0 copy-start.2
  36.9 1.9 copy-done.2
  38.8 1.0 fusion.3
  39.8 0.0 copy-done.4
  39.8 0.2 copy.26
  40.0 3.3 %fusion.17 = bf16[128,2,4,128]{0,3,2,1:T(8,128)(2,1)S(1)} fusion(bf16[1024,2,128,1]{0,2,3,1:T(8,128)(2,1)S(1)} %bitcast.65, f32[2,1024,128,4]{2,1,3,0:T(8,128)} %copy-done.2, f32[128,2,4]{0,2,1:T(4,128)S(1)} %broadcast_maximum_fusion, pred[128,1024]{0,1:T(8,128)(4,1)S(1)} %compare_and_fusion, f32[128,2,4]{0,2,1:T(4,128)S(1)} %fusion.3), kind=kOutput, calls=%fused_computation.18 | convolution fusion | flops 273940480 | bytes 5120000 | tf_op jit(solution)/shard_map/tkgn,nkd->tkgd/dot_general | solution.py:579
  43.4 0.2 copy.32
  43.6 0.2 dot_general.25
  43.8 6.0 %fusion.part_ref = f32[4,32,4096]{2,1,0:T(8,128)} fusion(bf16[4,32,1024]{2,1,0:T(8,128)(2,1)S(1)} %dot_general.25, bf16[1024,4096]{1,0:T(8,128)(2,1)} %param.18), kind=kOutput, calls=%fused_computation | convolution fusion | flops 1073741824 | bytes 10747904 | tf_op jit(solution)/shard_map/dot_general | solution.py:590
  49.8 0.0 copy-start.6
  49.8 117.5 %shard_map.128 = (f32[1024,2048]{1,0:T(8,128)}, f32[1024,2048]{1,0:T(8,128)}, f32[8,1024]{1,0:T(8,128)}) custom-call(f32[4,32,4096]{2,1,0:T(8,128)} %fusion.part_ref, bf16[4,32,4096]{2,1,0:T(8,128)(2,1)} %bitcast.58, f32[1,4096]{1,0:T(1,128)} %bitcast.68, bf16[4,32,2048]{2,1,0:T(8,128)(2,1)} %bitcast.64, bf16[2048,4096]{1,0:T(8,128)(2,1)} %t_head.1, ...), custom_call_target="tpu_custom_call" | custom-call | tf_op jit(solution)/shard_map/pallas_call | solution.py:170
  167.3 0.0 copy-done.6
  167.3 0.6 convert_element_type.48
  167.9 0.0 copy-start.1
  167.9 40.5 %shard_map.129 = f32[128,512]{1,0:T(8,128)} custom-call(f32[8,1024]{1,0:T(8,128)} %get-tuple-element.8.totals_ref, f32[1,1024]{1,0:T(1,128)} %bitcast.69, f32[1024,2048]{1,0:T(8,128)} %get-tuple-element.9.t_logits, f32[1024,2048]{1,0:T(8,128)} %get-tuple-element.10.d_logits, bf16[2048,2048]{1,0:T(8,128)(2,1)} %d_head.3), custom_call_target="tpu_custom_call" | custom-call | tf_op jit(solution)/shard_map/pallas_call | solution.py:170
  208.3 1.7 copy.44
  210.0 0.0 copy-done.1
  (10 shorter events, 0.1 us)
Async XLA Ops:
  0.0 2.8 %copy-start = (bf16[4096,256]{1,0:T(8,128)(2,1)S(1)}, bf16[4096,256]{1,0:T(8,128)(2,1)}, u32[]{:S(2)}) copy-start(bf16[4096,256]{1,0:T(8,128)(2,1)} %param.16) | copy-start | bytes 6291460
  0.0 5.1 %copy-start.3 = (bf16[128,4096]{1,0:T(8,128)(2,1)S(1)}, bf16[128,4096]{1,0:T(8,128)(2,1)}, u32[]{:S(2)}) copy-start(bf16[128,4096]{1,0:T(8,128)(2,1)} %param.13) | copy-start | bytes 3145732
  0.0 5.1 %copy-start.5 = (f32[4096]{0:T(1024)S(1)}, f32[4096]{0:T(1024)}, u32[]{:S(2)}) copy-start(f32[4096]{0:T(1024)} %param.14) | copy-start | bytes 49156
  5.1 24.8 %copy-start.8 = (s32[4]{0:T(128)S(1)}, s32[4]{0:T(128)}, u32[]{:S(2)}) copy-start(s32[4]{0:T(128)} %param.24) | copy-start | bytes 52
  5.1 25.1 %copy-start.7 = (s32[16]{0:T(128)S(1)}, s32[16]{0:T(128)}, u32[]{:S(2)}) copy-start(s32[16]{0:T(128)} %param.25) | copy-start | bytes 196
  35.9 3.9 %copy-start.4 = (bf16[1024,256]{1,0:T(8,128)(2,1)S(1)}, bf16[1024,256]{1,0:T(8,128)(2,1)}, u32[]{:S(2)}) copy-start(bf16[1024,256]{1,0:T(8,128)(2,1)} %get-tuple-element.14) | copy-start | bytes 1572868
  36.9 1.9 copy-start.2
  49.8 117.5 %copy-start.6 = (s32[1024]{0:T(1024)S(1)}, s32[1024]{0:T(1024)}, u32[]{:S(2)}) copy-start(s32[1024]{0:T(1024)} %param.23) | copy-start | bytes 12292
  167.9 42.2 %copy-start.1 = (bf16[4096,256]{1,0:T(8,128)(2,1)S(1)}, bf16[4096,256]{1,0:T(8,128)(2,1)}, u32[]{:S(2)}) copy-start(bf16[4096,256]{1,0:T(8,128)(2,1)} %param.16) | copy-start | bytes 6291460

commit v3 on v2

--- a/solution.py
+++ b/solution.py
@@ -179,23 +179,75 @@
     )(*operands)
 
 
-def gather_context_body(chips, own_ref, out_ref, *sems):
+def halves(rows):
+    width = rows.shape[-1] // 2
+    return lambda c, v, half: rows.at[c, v, :, half * width : (half + 1) * width]
+
+
+def context_body(
+    chips, peers, own_ref, query_ref, q_pos, q_roll, k_pos, k_roll, draft_ref,
+    attended_ref, draft_all, context, mask, *sems,
+):
     ctx, vocab, core, chip, sibling = place()
-    width = own_ref.shape[1] // 2
+    half_width = own_ref.shape[1] // 2
+    tokens = mask.shape[1]
+    heads = query_ref.shape[1] // HEAD_DIM
+    group_size = heads // (half_width // HEAD_DIM)
     greet(
         [(sibling, vocab)]
         + [(((chip + far) % chips) * 2 + core, vocab) for far in range(1, chips)]
-    )
-    out_ref[ctx] = own_ref[...]
+        + [(ctx, (vocab + far) % peers) for far in range(1, peers)]
+    )
+    context[ctx] = own_ref[...]
     blocks = Spread(
-        chips, 1, lambda c, v, half: out_ref.at[c, :, half * width : (half + 1) * width], sems
+        chips,
+        1,
+        lambda c, v, half: context.at[c, :, half * half_width : (half + 1) * half_width],
+        sems[:6],
     )
     blocks.start()
+    draft_all[ctx, vocab] = draft_ref[vocab]
+    draft = Spread(chips, peers, halves(draft_all), sems[6:])
+    draft.start()
+    allowed = (k_pos[...] <= q_pos[...]) & (k_roll[...] == q_roll[...])
+    mask[...] = jnp.where(allowed, 1.0, 0.0)
     for step in blocks.steps():
         blocks.step(step)
+    pending = list(draft.steps())
+    for step in pending[: chips - 1]:
+        draft.step(step)
+    pending = pending[chips - 1 :]
     for far in range(chips):
         blocks.collect(far)
+    for head in range(heads):
+        at = slice(head * HEAD_DIM, (head + 1) * HEAD_DIM)
+        begin = (head // group_size) * HEAD_DIM
+        keys = context[:, :, begin : begin + HEAD_DIM].reshape(tokens, HEAD_DIM)
+        values = context[:, :, half_width + begin : half_width + begin + HEAD_DIM].reshape(
+            tokens, HEAD_DIM
+        )
+        scores = lax.dot_general(
+            query_ref[:, at],
+            keys,
+            (((1,), (1,)), ((), ())),
+            preferred_element_type=jnp.float32,
+        ) * (HEAD_DIM ** (-0.5))
+        scores = jnp.where(mask[...] > 0.0, scores, NEGATIVE)
+        weights = jnp.exp(scores - jnp.max(scores, axis=1, keepdims=True))
+        weighted = jnp.dot(
+            weights.astype(jnp.bfloat16), values, preferred_element_type=jnp.float32
+        )
+        attended_ref[:, at] = (weighted / jnp.sum(weights, axis=1, keepdims=True)).astype(
+            jnp.bfloat16
+        )
+        if pending and head % 2 == 1:
+            draft.step(pending.pop(0))
+    for step in pending:
+        draft.step(step)
+    for far in range(chips):
+        draft.collect(far)
     blocks.finish()
+    draft.finish()
 
 
 def combine_pairs(former, latter):
@@ -210,13 +262,8 @@
     return merged
 
 
-def halves(rows):
-    width = rows.shape[-1] // 2
-    return lambda c, v, half: rows.at[c, v, :, half * width : (half + 1) * width]
-
-
 def logits_body(
-    chips, peers, part_ref, hidden_ref, gain_ref, draft_ref, t_head, d_head,
+    chips, peers, part_ref, hidden_ref, gain_ref, draft_from, t_head, d_head,
     t_out, d_out, totals_ref,
     final_all, draft_all, t_words, d_words, slots, columns, held, landed, send_buf, recv_buf,
     load_sem, store_sem, r_send, r_recv, x_send, x_recv, *sems,
@@ -229,7 +276,8 @@
     ]
     loads = [
         pltpu.make_async_copy(d_head, d_words, load_sem.at[0]),
-        pltpu.make_async_copy(t_head, t_words, load_sem.at[1]),
+        pltpu.make_async_copy(draft_from, draft_all, load_sem.at[1]),
+        pltpu.make_async_copy(t_head, t_words, load_sem.at[2]),
     ]
     for load in loads:
         load.start()
@@ -248,22 +296,7 @@
             )
         )
         copies[-1].start()
-    draft_all[ctx, vocab] = draft_ref[vocab]
-    draft = Spread(chips, peers, halves(draft_all), sems[:6])
-    teacher = Spread(chips, peers, halves(final_all), sems[6:])
-    draft.start()
-    for step in range(1, chips):
-        draft.step(step)
-    for copy in copies:
-        copy.wait_recv()
-    mixed = hidden_ref[vocab].astype(jnp.float32) + part_ref[vocab]
-    for far in range(1, peers):
-        mixed = mixed + recv_buf[far - 1].astype(jnp.float32)
-    final_all[ctx, vocab] = rms_scale(mixed, gain_ref[...]).astype(jnp.bfloat16)
-    teacher.start()
-    for step in draft.steps():
-        if step >= chips:
-            draft.step(step)
+    teacher = Spread(chips, peers, halves(final_all), sems)
 
     rows, words = slots.shape[1], slots.shape[2]
     tile = min(words, 512)
@@ -274,7 +307,8 @@
     def multiply(blocks, source_ref, head_ref, out_ref, member, far):
         count = len(stores)
         slot = count % 2
-        blocks.collect(far)
+        if blocks is not None:
+            blocks.collect(far)
         owner = (chip - far + chips) % chips
         if count >= 2:
             stores[count - 2].wait()
@@ -313,21 +347,38 @@
         for which in (0, 1):
             held[0, member + which : member + which + 1, lanes] = jnp.transpose(columns[which])[:1]
 
-    for load in loads:
-        load.wait()
-    done = [0, 0]
+    def draft_unit(far):
+        multiply(None, draft_all, d_words, d_out, 2, far)
+
+    def teacher_unit(far):
+        multiply(teacher, final_all, t_words, t_out, 0, far)
+
+    loads[0].wait()
+    loads[1].wait()
+    early = (chips + 1) // 2
+    for far in range(early):
+        draft_unit(far)
+    for copy in copies:
+        copy.wait_recv()
+    mixed = hidden_ref[vocab].astype(jnp.float32) + part_ref[vocab]
+    for far in range(1, peers):
+        mixed = mixed + recv_buf[far - 1].astype(jnp.float32)
+    final_all[ctx, vocab] = rms_scale(mixed, gain_ref[...]).astype(jnp.bfloat16)
+    teacher.start()
+    loads[2].wait()
+    waiting = list(range(early, chips))
+    done = 0
     for step in teacher.steps():
         teacher.step(step)
-        if done[0] < chips:
-            multiply(draft, draft_all, d_words, d_out, 2, done[0])
-            done[0] += 1
+        if waiting:
+            draft_unit(waiting.pop(0))
         if step > len(teacher.bits):
-            multiply(teacher, final_all, t_words, t_out, 0, done[1])
-            done[1] += 1
-    for far in range(done[0], chips):
-        multiply(draft, draft_all, d_words, d_out, 2, far)
-    for far in range(done[1], chips):
-        multiply(teacher, final_all, t_words, t_out, 0, far)
+            teacher_unit(done)
+            done += 1
+    for far in waiting:
+        draft_unit(far)
+    for far in range(done, chips):
+        teacher_unit(far)
 
     state = [held[0, member : member + 1] for member in range(4)]
     slot, x_copies = 0, []
@@ -352,7 +403,6 @@
         totals_ref[member : member + 1] = state[member]
     for copy in copies + x_copies:
         copy.wait_send()
-    draft.finish()
     teacher.finish()
     for store in stores[-2:]:
         store.wait()
@@ -552,46 +602,37 @@
     )
     keys = rotate(keys, query_pos).astype(jnp.bfloat16).reshape(row_count, local_groups * head_dim)
     values = jnp.dot(normed, w_value, preferred_element_type=jnp.float32).astype(jnp.bfloat16)
-    score_scale = head_dim ** (-0.5)
     own = jnp.concatenate([keys, values], axis=1)
-    gathered = communicate(
-        functools.partial(gather_context_body, chips),
-        [jax.ShapeDtypeStruct((ctx_count,) + own.shape, bf16)],
-        (own,),
-        spread_sems(chips, 1),
+    features = draft_rows.shape[1]
+    share = row_count // peers
+    tokens = row_count * ctx_count
+    key_pos, key_roll = locate(jnp.int32(0), tokens)
+    attended, draft_all = communicate(
+        functools.partial(context_body, chips, peers),
+        [
+            jax.ShapeDtypeStruct((row_count, local_heads * head_dim), bf16),
+            jax.ShapeDtypeStruct((ctx_count, peers, share, features), bf16),
+        ],
+        (
+            own,
+            queries.reshape(row_count, local_heads * head_dim),
+            query_pos[:, None],
+            query_roll[:, None],
+            key_pos[None, :],
+            key_roll[None, :],
+            draft_rows.reshape(peers, share, features),
+        ),
+        [
+            pltpu.VMEM((ctx_count,) + own.shape, bf16),
+            pltpu.VMEM((row_count, tokens), f32),
+        ]
+        + spread_sems(chips, 1)
+        + spread_sems(chips, peers),
         0,
-    )[0].reshape(-1, own.shape[1])
-    key_piece = gathered[:, : keys.shape[1]].reshape(-1, local_groups, head_dim)
-    value_piece = gathered[:, keys.shape[1] :].reshape(-1, local_groups, head_dim)
-    key_count = key_piece.shape[0]
-    key_pos, key_roll = locate(jnp.int32(0), key_count)
-    allowed = (key_pos[None, :] <= query_pos[:, None]) & (key_roll[None, :] == query_roll[:, None])
-    running_max = jnp.full((row_count, local_groups, group_size), NEGATIVE, jnp.float32)
-    visible = allowed[:, None, None, :]
-    scores = (
-        jnp.einsum("tkgd,nkd->tkgn", queries, key_piece, preferred_element_type=jnp.float32)
-        * score_scale
-    )
-    scores = jnp.where(visible, scores, NEGATIVE)
-    new_max = jnp.maximum(running_max, jnp.max(scores, axis=-1))
-    weights = jnp.where(visible, jnp.exp(scores - new_max[..., None]), 0.0)
-    new_sum = jnp.sum(weights, axis=-1)
-    new_weighted = jnp.einsum(
-        "tkgn,nkd->tkgd",
-        weights.astype(jnp.bfloat16),
-        value_piece,
-        preferred_element_type=jnp.float32,
-    )
-    attended = (
-        (new_weighted / new_sum[..., None])
-        .astype(jnp.bfloat16)
-        .reshape(row_count, local_heads * head_dim)
     )
     partial_value = jnp.dot(attended, w_out, preferred_element_type=jnp.float32)
     width = hidden_in.shape[1]
-    share = row_count // peers
-    word_count, features = draft_head.shape
-    tokens = row_count * ctx_count
+    word_count = draft_head.shape[0]
     unit = 2 * row_count
     hops = 1 + (peers - 1) + (chips - 1)
     logits = jax.ShapeDtypeStruct((tokens, word_count), f32)
@@ -602,7 +643,7 @@
             partial_value.reshape(peers, share, width),
             hidden_in.reshape(peers, share, width),
             final_gain.reshape(1, width),
-            draft_rows.reshape(peers, share, features),
+            draft_all,
             teacher_head,
             draft_head,
         ),
@@ -617,17 +658,16 @@
             pltpu.VMEM((hops, 8, tokens), f32),
             pltpu.VMEM((peers - 1, share, width), bf16),
             pltpu.VMEM((peers - 1, share, width), bf16),
-            dma((2,)),
+            dma((3,)),
             dma((2 * chips,)),
             dma((peers - 1,)),
             dma((peers - 1,)),
             dma((hops,)),
             dma((hops,)),
         ]
-        + spread_sems(chips, peers)
         + spread_sems(chips, peers),
         1,
-        [pltpu.VMEM] * 4 + [pl.ANY] * 2,
+        [pltpu.VMEM] * 3 + [pl.ANY] * 3,
         [pl.ANY, pl.ANY, pltpu.VMEM],
     )
     slice_width = features // peers

time: 210 us -> 210 us (level)
  Pallas kernels: 178 us -> 184 us
  matrix products: 18.8 us -> 14.7 us
  local copies, waits for them, and re-layouts: 6.7 us -> 3.48 us
    pallas_call x3, Pallas kernels: 178 us -> 184 us  [communicate(): pl.pallas_call(body, out_shape=out_shape, in_specs=[pl.BlockSpec(memory_s...]
    dot_general x2 -> x0, matrix products: 4.3 us -> none  [the longest x1 3.33 us: on_device(): jnp.einsum('tkgn,nkd->tkgd', weights.astype(jnp.bfloat16), value_piece, p...]
    slice x2 -> x0, local copies, waits for them, and re-layouts: 2.27 us -> none  [the longest x1 2.06 us: on_device(): key_piece = gathered[:, :keys.shape[1]].reshape(-1, local_groups, head_dim)]
where the time goes in v3:
time: 210 us; the launch traced here: 209 us
  Pallas kernels  184 us (88%)
  matrix products  14.7 us (7%)
  other arithmetic  7.25 us (3%)
  local copies, waits for them, and re-layouts  3.48 us (2%)
    pallas_call x3, Pallas kernels, communicate(): pl.pallas_call(body, out_shape=out_shape, in_specs=[pl.BlockSpec(memory_s...  184 us
    dot_general x1, matrix products, on_device(): partial_value = jnp.dot(attended, w_out, preferred_element_type=jnp.float32)  6.08 us
    dot_general x1, matrix products, on_device(): jnp.dot(normed, w_query, preferred_element_type=jnp.float32)  4.72 us

profile of v3, /device:TPU:0, one launch (start us, length us, event | category | flops | bytes accessed | tf_op | source)
XLA Modules:
  0.0 209.4 jit_solution(16606341157647378874)
XLA Ops:
  0.0 0.0 copy-start
  0.0 0.9 select_reduce_fusion.1
  0.9 0.3 multiply_cosine_fusion
  1.2 1.5 fusion
  2.8 0.0 copy-done
  2.8 0.0 copy-start.2
  2.8 0.0 copy-start.3
  2.8 1.8 fusion.20
  4.6 0.1 reshape.248
  4.7 0.3 subtract_convert_fusion.1
  5.0 0.2 pad_maximum_fusion.2
  5.2 0.0 copy-done.2
  5.2 0.0 copy-done.3
  5.2 2.1 %convolution_convert_fusion = bf16[128,256]{1,0:T(8,128)(2,1)S(1)} fusion(bf16[4096,256]{1,0:T(8,128)(2,1)} %param.17, bf16[128,4096]{1,0:T(8,128)(2,1)S(1)} %copy-done.2, f32[4096]{0:T(1024)S(1)} %copy-done.3, f32[128]{0:T(128)S(1)} %add_rsqrt_fusion), kind=kOutput, calls=%fused_computation.6 | convolution fusion | flops 270565376 | bytes 3228160 | tf_op jit(solution)/shard_map/dot_general | solution.py:604
  7.3 0.7 pad_maximum_fusion.1.own_ref
  8.0 4.7 %convolution_bitcast_fusion = f32[16,8,8,128]{3,1,2,0:T(8,128)S(1)} fusion(bf16[4096,1024]{1,0:T(8,128)(2,1)} %param.15, bf16[128,4096]{1,0:T(8,128)(2,1)S(1)} %copy-done.2, f32[4096]{0:T(1024)S(1)} %copy-done.3, f32[128]{0:T(128)S(1)} %add_rsqrt_fusion), kind=kOutput, calls=%fused_computation.5 | convolution fusion | flops 1075838976 | bytes 9978368 | tf_op jit(solution)/shard_map/dot_general | solution.py:592
  12.7 0.0 copy-start.6
  12.8 0.0 copy-start.5
  12.8 0.1 copy.19
  12.9 0.3 subtract_convert_fusion
  13.2 0.1 pad_maximum_fusion
  13.3 0.8 copy.23
  14.1 0.1 copy.16
  14.2 0.7 fusion.4.q_pos
  14.9 0.0 copy-done.6
  14.9 0.2 reduce-window.8
  15.0 0.1 convert_reduce_fusion.1
  15.1 0.7 copy.17.q_roll
  15.9 0.0 copy-done.5
  15.9 0.1 select_reduce_fusion
  16.0 0.7 convert_reduce_fusion
  16.6 0.6 fusion.14.k_pos
  17.2 46.8 %shard_map.127 = (bf16[128,1024]{1,0:T(8,128)(2,1)}, bf16[8,4,32,2048]{3,2,1,0:T(8,128)(2,1)}) custom-call(bf16[128,512]{1,0:T(8,128)(2,1)} %pad_maximum_fusion.1.own_ref, bf16[128,1024]{1,0:T(8,128)(2,1)} %bitcast.32, s32[128,1]{1,0:T(8,128)} %fusion.4.q_pos, s32[128,1]{1,0:T(8,128)} %copy.17.q_roll, s32[1,1024]{1,0:T(1,128)} %fusion.14.k_pos, ...), custom_call_target="tpu_custom_call" | custom-call | tf_op jit(solution)/shard_map/pallas_call | solution.py:170
  64.1 6.1 %fusion.24 = f32[128,4096]{1,0:T(8,128)} fusion(bf16[128,1024]{1,0:T(8,128)(2,1)} %get-tuple-element.10, bf16[1024,4096]{1,0:T(8,128)(2,1)} %param.18), kind=kOutput, calls=%fused_computation.59 | convolution fusion | flops 1073741824 | bytes 10747904 | tf_op jit(solution)/shard_map/dot_general | solution.py:633
  70.2 0.0 copy-start.4
  70.2 96.5 %shard_map.128 = (f32[1024,2048]{1,0:T(8,128)}, f32[1024,2048]{1,0:T(8,128)}, f32[8,1024]{1,0:T(8,128)}) custom-call(f32[4,32,4096]{2,1,0:T(8,128)} %bitcast.29, bf16[4,32,4096]{2,1,0:T(8,128)(2,1)} %bitcast.28, f32[1,4096]{1,0:T(1,128)} %bitcast.36, bf16[8,4,32,2048]{3,2,1,0:T(8,128)(2,1)} %get-tuple-element.11.draft_from, bf16[2048,4096]{1,0:T(8,128)(2,1)} %t_head.1, ...), custom_call_target="tpu_custom_call" | custom-call | tf_op jit(solution)/shard_map/pallas_call | solution.py:170
  166.6 0.0 copy-done.4
  166.6 0.6 convert_element_type.44
  167.2 0.0 copy-start.1
  167.2 40.5 %shard_map.129 = f32[128,512]{1,0:T(8,128)} custom-call(f32[8,1024]{1,0:T(8,128)} %get-tuple-element.12.totals_ref, f32[1,1024]{1,0:T(1,128)} %bitcast.39, f32[1024,2048]{1,0:T(8,128)} %get-tuple-element.13.t_logits, f32[1024,2048]{1,0:T(8,128)} %get-tuple-element.14.d_logits, bf16[2048,2048]{1,0:T(8,128)(2,1)} %d_head.3), custom_call_target="tpu_custom_call" | custom-call | tf_op jit(solution)/shard_map/pallas_call | solution.py:170
  207.7 1.7 copy.26
  209.4 0.0 copy-done.1
  (7 shorter events, 0.1 us)
Async XLA Ops:
  0.0 2.8 %copy-start = (bf16[4096,256]{1,0:T(8,128)(2,1)S(1)}, bf16[4096,256]{1,0:T(8,128)(2,1)}, u32[]{:S(2)}) copy-start(bf16[4096,256]{1,0:T(8,128)(2,1)} %param.16) | copy-start | bytes 6291460
  2.8 2.4 %copy-start.2 = (bf16[128,4096]{1,0:T(8,128)(2,1)S(1)}, bf16[128,4096]{1,0:T(8,128)(2,1)}, u32[]{:S(2)}) copy-start(bf16[128,4096]{1,0:T(8,128)(2,1)} %param.13) | copy-start | bytes 3145732
  2.8 2.4 %copy-start.3 = (f32[4096]{0:T(1024)S(1)}, f32[4096]{0:T(1024)}, u32[]{:S(2)}) copy-start(f32[4096]{0:T(1024)} %param.14) | copy-start | bytes 49156
  12.7 2.1 %copy-start.6 = (s32[4]{0:T(128)S(1)}, s32[4]{0:T(128)}, u32[]{:S(2)}) copy-start(s32[4]{0:T(128)} %param.24) | copy-start | bytes 52
  12.8 3.1 %copy-start.5 = (s32[16]{0:T(128)S(1)}, s32[16]{0:T(128)}, u32[]{:S(2)}) copy-start(s32[16]{0:T(128)} %param.25) | copy-start | bytes 196
  70.2 96.5 %copy-start.4 = (s32[1024]{0:T(1024)S(1)}, s32[1024]{0:T(1024)}, u32[]{:S(2)}) copy-start(s32[1024]{0:T(1024)} %param.23) | copy-start | bytes 12292
  167.2 42.1 %copy-start.1 = (bf16[4096,256]{1,0:T(8,128)(2,1)S(1)}, bf16[4096,256]{1,0:T(8,128)(2,1)}, u32[]{:S(2)}) copy-start(bf16[4096,256]{1,0:T(8,128)(2,1)} %param.16) | copy-start | bytes 6291460

commit v4 on v3

--- a/solution.py
+++ b/solution.py
@@ -185,14 +185,16 @@
 
 
 def context_body(
-    chips, peers, own_ref, query_ref, q_pos, q_roll, k_pos, k_roll, draft_ref,
-    attended_ref, draft_all, context, mask, *sems,
+    chips, peers, own_ref, query_ref, q_pos, q_roll, k_pos, k_roll, draft_ref, w_out,
+    part_ref, draft_all, context, mask, attended, w_held, load_sem, *sems,
 ):
     ctx, vocab, core, chip, sibling = place()
     half_width = own_ref.shape[1] // 2
     tokens = mask.shape[1]
     heads = query_ref.shape[1] // HEAD_DIM
     group_size = heads // (half_width // HEAD_DIM)
+    load = pltpu.make_async_copy(w_out, w_held, load_sem.at[0])
+    load.start()
     greet(
         [(sibling, vocab)]
         + [(((chip + far) % chips) * 2 + core, vocab) for far in range(1, chips)]
@@ -214,9 +216,7 @@
     for step in blocks.steps():
         blocks.step(step)
     pending = list(draft.steps())
-    for step in pending[: chips - 1]:
-        draft.step(step)
-    pending = pending[chips - 1 :]
+    draft.step(pending.pop(0))
     for far in range(chips):
         blocks.collect(far)
     for head in range(heads):
@@ -237,11 +237,22 @@
         weighted = jnp.dot(
             weights.astype(jnp.bfloat16), values, preferred_element_type=jnp.float32
         )
-        attended_ref[:, at] = (weighted / jnp.sum(weights, axis=1, keepdims=True)).astype(
+        attended[:, at] = (weighted / jnp.sum(weights, axis=1, keepdims=True)).astype(
             jnp.bfloat16
         )
         if pending and head % 2 == 1:
             draft.step(pending.pop(0))
+    load.wait()
+    tile = 512
+
+    def over_features(i, carry):
+        at = pl.ds(pl.multiple_of(i * tile, tile), tile)
+        part_ref[:, at] = jnp.dot(
+            attended[...], w_held[:, at], preferred_element_type=jnp.float32
+        )
+        return carry
+
+    lax.fori_loop(0, part_ref.shape[1] // tile, over_features, 0)
     for step in pending:
         draft.step(step)
     for far in range(chips):
@@ -607,10 +618,10 @@
     share = row_count // peers
     tokens = row_count * ctx_count
     key_pos, key_roll = locate(jnp.int32(0), tokens)
-    attended, draft_all = communicate(
+    partial_value, draft_all = communicate(
         functools.partial(context_body, chips, peers),
         [
-            jax.ShapeDtypeStruct((row_count, local_heads * head_dim), bf16),
+            jax.ShapeDtypeStruct((row_count, w_out.shape[1]), f32),
             jax.ShapeDtypeStruct((ctx_count, peers, share, features), bf16),
         ],
         (
@@ -621,16 +632,20 @@
             key_pos[None, :],
             key_roll[None, :],
             draft_rows.reshape(peers, share, features),
+            w_out,
         ),
         [
             pltpu.VMEM((ctx_count,) + own.shape, bf16),
             pltpu.VMEM((row_count, tokens), f32),
+            pltpu.VMEM((row_count, local_heads * head_dim), bf16),
+            pltpu.VMEM(w_out.shape, bf16),
+            dma((1,)),
         ]
         + spread_sems(chips, 1)
         + spread_sems(chips, peers),
         0,
-    )
-    partial_value = jnp.dot(attended, w_out, preferred_element_type=jnp.float32)
+        [pltpu.VMEM] * 7 + [pl.ANY],
+    )
     width = hidden_in.shape[1]
     word_count = draft_head.shape[0]
     unit = 2 * row_count

time: 210 us -> 204 us (0.971)
  matrix products: 14.7 us -> 8.63 us
    dot_general x1 -> x0, matrix products: 6.08 us -> none  [on_device(): partial_value = jnp.dot(attended, w_out, preferred_element_type=jnp.float32)]
where the time goes in v4:
time: 204 us
  Pallas kernels  184 us (90%)
  matrix products  8.63 us (4%)
  other arithmetic  7.24 us (4%)
  local copies, waits for them, and re-layouts  3.48 us (2%)
    pallas_call x3, Pallas kernels, communicate(): pl.pallas_call(body, out_shape=out_shape, in_specs=[pl.BlockSpec(memory_s...  184 us
    dot_general x1, matrix products, on_device(): jnp.dot(normed, w_query, preferred_element_type=jnp.float32)  4.72 us

profile of v4, /device:TPU:0, one launch (start us, length us, event | category | flops | bytes accessed | tf_op | source)
XLA Modules:
  0.0 203.9 jit_solution(5745509136353530278)
XLA Ops:
  0.0 0.0 copy-start
  0.0 0.9 select_reduce_fusion.1
  0.9 0.3 multiply_cosine_fusion
  1.2 1.5 fusion
  2.8 0.0 copy-done
  2.8 0.0 copy-start.2
  2.8 0.0 copy-start.3
  2.8 1.8 fusion.20
  4.6 0.1 reshape.248
  4.7 0.3 subtract_convert_fusion.1
  5.0 0.2 pad_maximum_fusion.2
  5.2 0.0 copy-done.2
  5.2 0.0 copy-done.3
  5.2 2.1 %convolution_convert_fusion = bf16[128,256]{1,0:T(8,128)(2,1)S(1)} fusion(bf16[4096,256]{1,0:T(8,128)(2,1)} %param.17, bf16[128,4096]{1,0:T(8,128)(2,1)S(1)} %copy-done.2, f32[4096]{0:T(1024)S(1)} %copy-done.3, f32[128]{0:T(128)S(1)} %add_rsqrt_fusion), kind=kOutput, calls=%fused_computation.6 | convolution fusion | flops 270565376 | bytes 3228160 | tf_op jit(solution)/shard_map/dot_general | solution.py:615
  7.3 0.6 pad_maximum_fusion.1.own_ref
  8.0 4.7 %convolution_bitcast_fusion = f32[16,8,8,128]{3,1,2,0:T(8,128)S(1)} fusion(bf16[4096,1024]{1,0:T(8,128)(2,1)} %param.15, bf16[128,4096]{1,0:T(8,128)(2,1)S(1)} %copy-done.2, f32[4096]{0:T(1024)S(1)} %copy-done.3, f32[128]{0:T(128)S(1)} %add_rsqrt_fusion), kind=kOutput, calls=%fused_computation.5 | convolution fusion | flops 1075838976 | bytes 9978368 | tf_op jit(solution)/shard_map/dot_general | solution.py:603
  12.7 0.0 copy-start.6
  12.7 0.0 copy-start.5
  12.7 0.1 copy.19
  12.9 0.3 subtract_convert_fusion
  13.2 0.1 pad_maximum_fusion
  13.3 0.8 copy.23
  14.1 0.1 copy.16
  14.2 0.7 fusion.4.q_pos
  14.8 0.0 copy-done.6
  14.8 0.2 reduce-window.8
  15.0 0.1 convert_reduce_fusion.1
  15.1 0.7 copy.17.q_roll
  15.8 0.0 copy-done.5
  15.8 0.1 select_reduce_fusion
  15.9 0.7 convert_reduce_fusion
  16.6 0.6 fusion.14.k_pos
  17.2 48.4 %shard_map.127 = (f32[128,4096]{1,0:T(8,128)}, bf16[8,4,32,2048]{3,2,1,0:T(8,128)(2,1)}) custom-call(bf16[128,512]{1,0:T(8,128)(2,1)} %pad_maximum_fusion.1.own_ref, bf16[128,1024]{1,0:T(8,128)(2,1)} %bitcast.29, s32[128,1]{1,0:T(8,128)} %fusion.4.q_pos, s32[128,1]{1,0:T(8,128)} %copy.17.q_roll, s32[1,1024]{1,0:T(1,128)} %fusion.14.k_pos, ...), custom_call_target="tpu_custom_call" | custom-call | tf_op jit(solution)/shard_map/pallas_call | solution.py:170
  65.6 0.0 copy-start.4
  65.6 95.5 %shard_map.128 = (f32[1024,2048]{1,0:T(8,128)}, f32[1024,2048]{1,0:T(8,128)}, f32[8,1024]{1,0:T(8,128)}) custom-call(f32[4,32,4096]{2,1,0:T(8,128)} %bitcast.28, bf16[4,32,4096]{2,1,0:T(8,128)(2,1)} %bitcast.26, f32[1,4096]{1,0:T(1,128)} %bitcast.34, bf16[8,4,32,2048]{3,2,1,0:T(8,128)(2,1)} %get-tuple-element.11.draft_from, bf16[2048,4096]{1,0:T(8,128)(2,1)} %t_head.1, ...), custom_call_target="tpu_custom_call" | custom-call | tf_op jit(solution)/shard_map/pallas_call | solution.py:170
  161.2 0.0 copy-done.4
  161.2 0.6 convert_element_type.44
  161.8 0.0 copy-start.1
  161.8 40.5 %shard_map.129 = f32[128,512]{1,0:T(8,128)} custom-call(f32[8,1024]{1,0:T(8,128)} %get-tuple-element.12.totals_ref, f32[1,1024]{1,0:T(1,128)} %bitcast.37, f32[1024,2048]{1,0:T(8,128)} %get-tuple-element.13.t_logits, f32[1024,2048]{1,0:T(8,128)} %get-tuple-element.14.d_logits, bf16[2048,2048]{1,0:T(8,128)(2,1)} %d_head.3), custom_call_target="tpu_custom_call" | custom-call | tf_op jit(solution)/shard_map/pallas_call | solution.py:170
  202.3 1.7 copy.26
  203.9 0.0 copy-done.1
  (7 shorter events, 0.1 us)
Async XLA Ops:
  0.0 2.8 %copy-start = (bf16[4096,256]{1,0:T(8,128)(2,1)S(1)}, bf16[4096,256]{1,0:T(8,128)(2,1)}, u32[]{:S(2)}) copy-start(bf16[4096,256]{1,0:T(8,128)(2,1)} %param.16) | copy-start | bytes 6291460
  2.8 2.4 %copy-start.2 = (bf16[128,4096]{1,0:T(8,128)(2,1)S(1)}, bf16[128,4096]{1,0:T(8,128)(2,1)}, u32[]{:S(2)}) copy-start(bf16[128,4096]{1,0:T(8,128)(2,1)} %param.13) | copy-start | bytes 3145732
  2.8 2.4 %copy-start.3 = (f32[4096]{0:T(1024)S(1)}, f32[4096]{0:T(1024)}, u32[]{:S(2)}) copy-start(f32[4096]{0:T(1024)} %param.14) | copy-start | bytes 49156
  12.7 2.1 %copy-start.6 = (s32[4]{0:T(128)S(1)}, s32[4]{0:T(128)}, u32[]{:S(2)}) copy-start(s32[4]{0:T(128)} %param.24) | copy-start | bytes 52
  12.7 3.1 %copy-start.5 = (s32[16]{0:T(128)S(1)}, s32[16]{0:T(128)}, u32[]{:S(2)}) copy-start(s32[16]{0:T(128)} %param.25) | copy-start | bytes 196
  65.6 95.6 %copy-start.4 = (s32[1024]{0:T(1024)S(1)}, s32[1024]{0:T(1024)}, u32[]{:S(2)}) copy-start(s32[1024]{0:T(1024)} %param.23) | copy-start | bytes 12292
  161.8 42.1 %copy-start.1 = (bf16[4096,256]{1,0:T(8,128)(2,1)S(1)}, bf16[4096,256]{1,0:T(8,128)(2,1)}, u32[]{:S(2)}) copy-start(bf16[4096,256]{1,0:T(8,128)(2,1)} %param.16) | copy-start | bytes 6291460
